TPU v7x, 32 devices: a whole 2x2x4 slice. The times are simulated.
32 devices in a mesh: dp: 16 (over z, y, core), shard: 2 (over x).
Axes of the slice: x: 2, y: 2, z: 4, core: 2. Of those that a mesh axis runs over, the one named last changes fastest.
Arguments:
- inputs: bfloat16 [16384, 1600], P(('dp', 'shard')), may hold values from -6 to 6
- cotangent: bfloat16 [16384, 1600], P(('dp', 'shard')), may hold values from -6 to 6
- seq_lengths: int32 [32, 4], P(('dp', 'shard')), may hold values from 0 to 512, as said below
- qkv_weight: float32 [1600, 4800], P('shard'), may hold values from -0.15625 to 0.15625
- out_weight: float32 [1600, 1600], P('shard'), may hold values from -0.625 to 0.625
- up_weight: float32 [1600, 6400], P('shard'), may hold values from -0.15625 to 0.15625
- down_weight: float32 [6400, 1600], P('shard'), may hold values from -0.078125 to 0.078125
- vector_params: float32 [19200], P('shard'), may hold values from -0.6 to 1.45, as said below
- qkv_momentum: float32 [1600, 4800], P('shard'), may hold values from -16 to 16
- out_momentum: float32 [1600, 1600], P('shard'), may hold values from -6 to 6
- up_momentum: float32 [1600, 6400], P('shard'), may hold values from -40 to 40
- down_momentum: float32 [6400, 1600], P('shard'), may hold values from -40 to 40
- vector_momentum: float32 [19200], P('shard'), may hold values from -64 to 64
- qkv_variance: float32 [1600, 4800], P('shard'), may hold values from 0.32768 to 2.62144
- out_variance: float32 [1600, 1600], P('shard'), may hold values from 0.1851392 to 1.47456
- up_variance: float32 [1600, 6400], P('shard'), may hold values from 2.048 to 16.384
- down_variance: float32 [6400, 1600], P('shard'), may hold values from 2.048 to 16.384
- vector_variance: float32 [19200], P('shard'), may hold values from 5.24288 to 41.94304
Outputs:
- layer_output: bfloat16 [16384, 1600], P(('dp', 'shard'))
- input_grad: bfloat16 [16384, 1600], P(('dp', 'shard'))
- updated_qkv: float32 [1600, 4800], P('shard')
- updated_out: float32 [1600, 1600], P('shard')
- updated_up: float32 [1600, 6400], P('shard')
- updated_down: float32 [6400, 1600], P('shard')
- updated_vector: float32 [19200], P('shard')
- momentum_qkv: float32 [1600, 4800], P('shard')
- momentum_out: float32 [1600, 1600], P('shard')
- momentum_up: float32 [1600, 6400], P('shard')
- momentum_down: float32 [6400, 1600], P('shard')
- momentum_vector: float32 [19200], P('shard')
- variance_qkv: float32 [1600, 4800], P('shard')
- variance_out: float32 [1600, 1600], P('shard')
- variance_up: float32 [1600, 6400], P('shard')
- variance_down: float32 [6400, 1600], P('shard')
- variance_vector: float32 [19200], P('shard')
Inputs may be any that keep to these rules, and one draw needn't show every extreme that they name: `seq_lengths`: on each device the blocks that its sequences take, ceil(length / 128) each, add up to at most 4. A zero is an empty entry. Some device holds a sequence of 512 tokens. `vector_params`: entries of the two gains lie near one, those of the biases near zero.
All inputs are finite; a program needn't handle non-finite values.
Results may differ from a plain program's by a relative error of at most 0.012.
The roundings to bfloat16 on the way count: a program that leaves them out, or rounds other values in their place, can miss the bound.
Values may be sent and summed in bfloat16 or wider, within the bound.
No kernel may reach another device: no remote copies, remote signals or barrier semaphores. Data moves between devices by JAX's collectives and lax.ppermute only.
A program may use at most 832 MiB of HBM per device.

v0:
```python
import jax
import jax.numpy as jnp
from jax import lax
from jax.sharding import PartitionSpec as P

HD = 64
BLK = 128
STEP = 10


NEG_FILL = -1e30
NORM_EPS = 1e-05
GELU_SCALE = 0.7978845608028654
BETA_ONE = 0.9
BETA_TWO = 0.999
LEARN_RATE = 0.06
VECTOR_RATE = 0.25
ADAM_EPS = 1e-08
WEIGHT_DECAY = 0.1


def layer_norm(values, gain_vec, shift_vec):
    center = values - jnp.mean(values, axis=-1, keepdims=True)
    spread = jnp.mean(center * center, axis=-1, keepdims=True)
    return center * lax.rsqrt(spread + NORM_EPS) * gain_vec + shift_vec


def gelu_tanh(values):
    return (
        0.5 * values * (1.0 + jnp.tanh(GELU_SCALE * (values + 0.044715 * values * values * values)))
    )


def layout(row_lengths, slot_count, block_size):
    blocks_used = (row_lengths + block_size - 1) // block_size
    starts = (jnp.cumsum(blocks_used) - blocks_used) * block_size
    position = jnp.arange(slot_count, dtype=jnp.int32)[:, None]
    inside = (position >= starts[None, :]) & (position < (starts + row_lengths)[None, :])
    labels = jnp.arange(row_lengths.shape[0], dtype=jnp.int32) + 1
    segment = jnp.sum(jnp.where(inside, labels[None, :], 0), axis=1) - 1
    return segment


def split_vector(vector, model_width, hidden):
    pieces = [vector[number * model_width : (number + 1) * model_width] for number in range(7)]
    bias_up = vector[7 * model_width : 7 * model_width + hidden]
    bias_down = vector[7 * model_width + hidden :]
    return pieces + [bias_up, bias_down]


def contract_rows(left_side, right_side):
    return lax.dot_general(
        left_side, right_side, (((0,), (0,)), ((), ())), preferred_element_type=jnp.float32
    )


def contract_cols(left_side, right_side):
    return lax.dot_general(
        left_side, right_side, (((1,), (1,)), ((), ())), preferred_element_type=jnp.float32
    )


def masked_scores(query_block, key_heads, seg_block, pos_block, segment, position):
    scores = (
        jnp.einsum("qhd,khd->hqk", query_block, key_heads, preferred_element_type=jnp.float32)
        * 0.125
    )
    allowed = (seg_block[:, None] == segment[None, :]) & (position[None, :] <= pos_block[:, None])
    return jnp.where(allowed[None], scores, NEG_FILL)


def attend_forward(queries, key_heads, values, segment):
    slot_count, head_count, head_size = queries.shape
    rows_block = min(512, slot_count)
    block_count = slot_count // rows_block
    position = jnp.arange(slot_count, dtype=jnp.int32)

    def one_block(block_item):
        query_block, seg_block, pos_block = block_item
        scores = masked_scores(query_block, key_heads, seg_block, pos_block, segment, position)
        row_max = jnp.max(scores, axis=-1, keepdims=True)
        exponent = jnp.exp(scores - row_max)
        totals = jnp.sum(exponent, axis=-1, keepdims=True)
        attn_probs = (exponent / totals).astype(jnp.bfloat16)
        result = jnp.einsum("hqk,khd->qhd", attn_probs, values, preferred_element_type=jnp.float32)
        return (result.astype(jnp.bfloat16), (row_max + jnp.log(totals))[..., 0])

    items = (
        queries.reshape(block_count, rows_block, head_count, head_size),
        segment.reshape(block_count, rows_block),
        position.reshape(block_count, rows_block),
    )
    attended, log_totals = lax.map(one_block, items)
    return (attended.reshape(slot_count, head_count * head_size), log_totals)


def attend_backward(queries, key_heads, values, segment, log_totals, grad_heads):
    slot_count, head_count, head_size = queries.shape
    rows_block = min(512, slot_count)
    block_count = slot_count // rows_block
    position = jnp.arange(slot_count, dtype=jnp.int32)

    def one_block(running, block_item):
        grad_keys, grad_values = running
        query_block, seg_block, pos_block, lse_block, gout_block = block_item
        scores = masked_scores(query_block, key_heads, seg_block, pos_block, segment, position)
        attn_probs = jnp.exp(scores - lse_block[..., None])
        probs_low = attn_probs.astype(jnp.bfloat16)
        grad_values = grad_values + jnp.einsum(
            "hqk,qhd->khd", probs_low, gout_block, preferred_element_type=jnp.float32
        )
        grad_probs = jnp.einsum(
            "qhd,khd->hqk", gout_block, values, preferred_element_type=jnp.float32
        )
        inner_sum = jnp.sum(grad_probs * attn_probs, axis=-1, keepdims=True)
        grad_scores = (attn_probs * (grad_probs - inner_sum)).astype(jnp.bfloat16)
        grad_query = (
            jnp.einsum("hqk,khd->qhd", grad_scores, key_heads, preferred_element_type=jnp.float32)
            * 0.125
        )
        grad_keys = (
            grad_keys
            + jnp.einsum(
                "hqk,qhd->khd", grad_scores, query_block, preferred_element_type=jnp.float32
            )
            * 0.125
        )
        return ((grad_keys, grad_values), grad_query)

    zero_heads = jnp.zeros((slot_count, head_count, head_size), jnp.float32)
    items = (
        queries.reshape(block_count, rows_block, head_count, head_size),
        segment.reshape(block_count, rows_block),
        position.reshape(block_count, rows_block),
        log_totals,
        grad_heads.reshape(block_count, rows_block, head_count, head_size),
    )
    (grad_keys, grad_values), grad_queries = lax.scan(one_block, (zero_heads, zero_heads), items)
    model_width = head_count * head_size
    return (
        grad_queries.reshape(slot_count, model_width),
        grad_keys.reshape(slot_count, model_width),
        grad_values.reshape(slot_count, model_width),
    )


def adamw_step(master, gradient, momentum, variance, decay_rate, step_rate):
    momentum_new = BETA_ONE * momentum + (1.0 - BETA_ONE) * gradient
    variance_new = BETA_TWO * variance + (1.0 - BETA_TWO) * gradient * gradient
    corrected_m = momentum_new / (1.0 - BETA_ONE**STEP)
    corrected_v = variance_new / (1.0 - BETA_TWO**STEP)
    updated = master - step_rate * (
        corrected_m / (jnp.sqrt(corrected_v) + ADAM_EPS) + decay_rate * master
    )
    return (updated, momentum_new, variance_new)


def local(
    inputs,
    cotangent,
    seq_lengths,
    qkv_weight,
    out_weight,
    up_weight,
    down_weight,
    vector_params,
    qkv_momentum,
    out_momentum,
    up_momentum,
    down_momentum,
    vector_momentum,
    qkv_variance,
    out_variance,
    up_variance,
    down_variance,
    vector_variance,
):
    slot_count, model_width = inputs.shape
    segment = layout(seq_lengths[0], slot_count, BLK)
    live_rows = (segment >= 0)[:, None]
    masters = (qkv_weight, out_weight, up_weight, down_weight, vector_params)
    lowered = tuple((master.astype(jnp.bfloat16) for master in masters))
    w_qkv, w_out, w_up, w_down, vector_low = (
        lax.all_gather(lowered[0], "shard", axis=0, tiled=True),
        lax.all_gather(lowered[1], "shard", axis=0, tiled=True),
        lax.all_gather(lowered[2], "shard", axis=0, tiled=True),
        lax.all_gather(lowered[3], "shard", axis=0, tiled=True),
        lax.all_gather(lowered[4], "shard", axis=0, tiled=True),
    )
    hidden = w_up.shape[1]
    head_count = model_width // HD
    vector = vector_low.astype(jnp.float32)
    (
        gain_one,
        shift_one,
        bias_query,
        bias_value,
        bias_out,
        gain_two,
        shift_two,
        bias_up,
        bias_down,
    ) = split_vector(vector, model_width, hidden)
    token_rows = inputs.astype(jnp.float32)
    normed = layer_norm(token_rows, gain_one, shift_one).astype(jnp.bfloat16)
    qkv_bias = jnp.concatenate([bias_query, jnp.zeros_like(bias_query), bias_value])
    projected = (jnp.dot(normed, w_qkv, preferred_element_type=jnp.float32) + qkv_bias).astype(
        jnp.bfloat16
    )
    queries = projected[:, :model_width].reshape(slot_count, head_count, HD)
    key_heads = projected[:, model_width : 2 * model_width].reshape(slot_count, head_count, HD)
    values = projected[:, 2 * model_width :].reshape(slot_count, head_count, HD)
    attended, log_totals = attend_forward(queries, key_heads, values, segment)
    residual = token_rows + jnp.dot(attended, w_out, preferred_element_type=jnp.float32) + bias_out
    normed_two = layer_norm(residual, gain_two, shift_two).astype(jnp.bfloat16)
    pre_act = jnp.dot(normed_two, w_up, preferred_element_type=jnp.float32) + bias_up
    activated = gelu_tanh(pre_act).astype(jnp.bfloat16)
    result = residual + jnp.dot(activated, w_down, preferred_element_type=jnp.float32) + bias_down
    layer_output = jnp.where(live_rows, result, 0.0).astype(jnp.bfloat16)
    grad_out = jnp.where(live_rows, cotangent.astype(jnp.float32), 0.0)
    grad_low = grad_out.astype(jnp.bfloat16)
    grad_down = contract_rows(activated, grad_low)
    bias_down_grad = jnp.sum(grad_low.astype(jnp.float32), axis=0)
    grad_activated = contract_cols(grad_low, w_down)
    _, gelu_pull = jax.vjp(gelu_tanh, pre_act)
    grad_pre = gelu_pull(grad_activated)[0].astype(jnp.bfloat16)
    grad_up = contract_rows(normed_two, grad_pre)
    bias_up_grad = jnp.sum(grad_pre.astype(jnp.float32), axis=0)
    grad_normed_two = contract_cols(grad_pre, w_up)
    _, second_pull = jax.vjp(layer_norm, residual, gain_two, shift_two)
    grad_resid_norm, gain_two_grad, shift_two_grad = second_pull(grad_normed_two)
    grad_residual = grad_out + grad_resid_norm
    grad_branch = grad_residual.astype(jnp.bfloat16)
    grad_out_w = contract_rows(attended, grad_branch)
    bias_out_grad = jnp.sum(grad_branch.astype(jnp.float32), axis=0)
    grad_attended = contract_cols(grad_branch, w_out).astype(jnp.bfloat16)
    grad_queries, grad_keys, grad_values = attend_backward(
        queries,
        key_heads,
        values,
        segment,
        log_totals,
        grad_attended.reshape(slot_count, head_count, HD),
    )
    grad_projected = jnp.concatenate([grad_queries, grad_keys, grad_values], axis=1).astype(
        jnp.bfloat16
    )
    grad_qkv_w = contract_rows(normed, grad_projected)
    column_sums = jnp.sum(grad_projected.astype(jnp.float32), axis=0)
    grad_normed = contract_cols(grad_projected, w_qkv)
    _, first_pull = jax.vjp(layer_norm, token_rows, gain_one, shift_one)
    grad_rows_norm, gain_one_grad, shift_one_grad = first_pull(grad_normed)
    input_grad = (grad_residual + grad_rows_norm).astype(jnp.bfloat16)
    grad_vector = jnp.concatenate(
        [
            gain_one_grad,
            shift_one_grad,
            column_sums[:model_width],
            column_sums[2 * model_width :],
            bias_out_grad,
            gain_two_grad,
            shift_two_grad,
            bias_up_grad,
            bias_down_grad,
        ]
    )
    shares = (
        lax.psum_scatter(grad_qkv_w, "shard", scatter_dimension=0, tiled=True),
        lax.psum_scatter(grad_out_w, "shard", scatter_dimension=0, tiled=True),
        lax.psum_scatter(grad_up, "shard", scatter_dimension=0, tiled=True),
        lax.psum_scatter(grad_down, "shard", scatter_dimension=0, tiled=True),
        lax.psum_scatter(grad_vector, "shard", scatter_dimension=0, tiled=True),
    )
    reduced = lax.psum((shares[0], shares[1], shares[2], shares[3], shares[4]), "dp")
    new_qkv = adamw_step(
        qkv_weight, reduced[0], qkv_momentum, qkv_variance, WEIGHT_DECAY, LEARN_RATE
    )
    new_out = adamw_step(
        out_weight, reduced[1], out_momentum, out_variance, WEIGHT_DECAY, LEARN_RATE
    )
    new_up = adamw_step(up_weight, reduced[2], up_momentum, up_variance, WEIGHT_DECAY, LEARN_RATE)
    new_down = adamw_step(
        down_weight, reduced[3], down_momentum, down_variance, WEIGHT_DECAY, LEARN_RATE
    )
    new_vector = adamw_step(
        vector_params, reduced[4], vector_momentum, vector_variance, 0.0, VECTOR_RATE
    )
    return (
        layer_output,
        input_grad,
        new_qkv[0],
        new_out[0],
        new_up[0],
        new_down[0],
        new_vector[0],
        new_qkv[1],
        new_out[1],
        new_up[1],
        new_down[1],
        new_vector[1],
        new_qkv[2],
        new_out[2],
        new_up[2],
        new_down[2],
        new_vector[2],
    )


def solution(mesh):
    return jax.shard_map(
        local,
        mesh=mesh,
        in_specs=(
            P(("dp", "shard"), None),
            P(("dp", "shard"), None),
            P(("dp", "shard"), None),
            P("shard", None),
            P("shard", None),
            P("shard", None),
            P("shard", None),
            P("shard"),
            P("shard", None),
            P("shard", None),
            P("shard", None),
            P("shard", None),
            P("shard"),
            P("shard", None),
            P("shard", None),
            P("shard", None),
            P("shard", None),
            P("shard"),
        ),
        out_specs=(
            P(("dp", "shard"), None),
            P(("dp", "shard"), None),
            P("shard", None),
            P("shard", None),
            P("shard", None),
            P("shard", None),
            P("shard"),
            P("shard", None),
            P("shard", None),
            P("shard", None),
            P("shard", None),
            P("shard"),
            P("shard", None),
            P("shard", None),
            P("shard", None),
            P("shard", None),
            P("shard"),
        ),
        check_vma=False,
    )
```

profile of v0, /device:TPU:0, one launch (start us, length us, event | category | flops | bytes accessed | tf_op | source)
XLA Modules:
  0.0 3398.9 jit_solution(6265885537286980704)
XLA Ops:
  7.2 9.4 convert_element_type.90
  16.7 4.3 convert_element_type.95
  21.0 14.1 convert_element_type.97
  35.2 13.0 convert_element_type.99
  49.1 6.2 all-gather
  57.8 147.8 %all-gather.6.cloned.1.call-done = bf16[1600,4800]{1,0:T(8,128)(2,1)} async-done(((bf16[800,4800]{1,0:T(8,128)(2,1)}), bf16[1600,4800]{1,0:T(8,128)(2,1)}) %all-gather.6.cloned.1.call-update) | async-done | bytes 15360016 | tf_op jit(solution)/shard_map/all_gather | solution.py:184
  205.5 14.7 add_convert_fusion
  220.6 11.0 fusion.66
  231.6 10.8 fusion
  242.4 12.4 fusion.31
  254.8 22.3 all-gather.8.cloned.1.call-done
  277.2 6.5 fusion.67
  283.7 1.7 copy-done.7
  285.8 235.6 %all-gather.10.cloned.1.call-done = bf16[1600,6400]{1,0:T(8,128)(2,1)} async-done(((bf16[800,6400]{1,0:T(8,128)(2,1)}), bf16[1600,6400]{1,0:T(8,128)(2,1)}) %all-gather.10.cloned.1.call-update) | async-done | bytes 20480016 | tf_op jit(solution)/shard_map/all_gather | solution.py:186
  521.3 21.5 convolution_add_fusion
  542.8 222.4 %all-gather.12.cloned.1.call-done = bf16[6400,1600]{0,1:T(8,128)(2,1)} async-done(((bf16[3200,1600]{0,1:T(8,128)(2,1)}), bf16[6400,1600]{0,1:T(8,128)(2,1)}) %all-gather.12.cloned.1.call-update) | async-done | bytes 20480016 | tf_op jit(solution)/shard_map/all_gather | solution.py:187
  765.3 30.7 convert_reduce_fusion
  795.9 20.5 multiply_reduce_fusion.1
  816.4 0.8 fusion.62
  817.3 1.7 copy-done
  818.9 1.3 convert_reduce_fusion.4
  820.2 1.2 copy-done.16
  821.4 5.8 fusion.68
  827.3 6.2 convolution_convert_fusion
  833.5 17.4 multiply_reduce_fusion
  850.9 22.8 multiply_convert_fusion
  873.7 10.0 multiply_convert_fusion.2
  883.7 7.2 multiply_convert_fusion.3
  891.0 14.6 fusion.32
  905.6 17.3 fusion.50
  923.0 22.5 fusion.35
  946.2 23.3 fusion.54
  969.5 19.1 fusion.55
  988.7 1.6 fusion.25
  990.3 1.5 convert_reduce_fusion.1
  991.8 2.9 convert_reduce_fusion.3
  994.8 0.7 concatenate.12
  995.6 301.0 %reduce-scatter.7.cloned.1.call-done = f32[800,4800]{1,0:T(8,128)} async-done(((f32[1600,4800]{1,0:T(8,128)}), f32[800,4800]{1,0:T(8,128)}) %reduce-scatter.7.cloned.1.call-update) | async-done | bytes 15360016 | tf_op jit(solution)/shard_map/reduce_scatter | solution.py:268
  1296.6 451.5 %reduce-scatter.11.cloned.1.call-done = f32[3200,1600]{0,1:T(8,128)} async-done(((f32[6400,1600]{0,1:T(8,128)}), f32[3200,1600]{0,1:T(8,128)}) %reduce-scatter.11.cloned.1.call-update) | async-done | bytes 20480016 | tf_op jit(solution)/shard_map/reduce_scatter | solution.py:271
  1748.2 451.5 %reduce-scatter.13.cloned.1.call-done = f32[800,6400]{1,0:T(8,128)} async-done(((f32[1600,6400]{1,0:T(8,128)}), f32[800,6400]{1,0:T(8,128)}) %reduce-scatter.13.cloned.1.call-update) | async-done | bytes 20480016
  2201.6 21.6 select_convert_fusion
  2223.4 0.9 dynamic-slice.4
  2224.3 64.6 %psum.39 = f32[9600]{0:T(1024)S(1)} all-reduce(f32[9600]{0:T(1024)S(1)} %dynamic-slice.4), channel_id=1, replica_groups=mesh['dp'=16,'shard'=2] {'dp'}, use_global_device_ids=true, to_apply=%region_30.31 | all-reduce | flops 9600 | bytes 76800 | tf_op jit(solution)/shard_map/psum | solution.py:274
  2289.6 951.9 %all-reduce.8.cloned.1.call-done = (f32[800,4800]{1,0:T(8,128)}, f32[800,1600]{1,0:T(8,128)}, f32[800,6400]{1,0:T(8,128)}, f32[3200,1600]{0,1:T(8,128)}) async-done(((f32[800,4800]{1,0:T(8,128)}, f32[800,1600]{1,0:T(8,128)}, f32[800,6400]{1,0:T(8,128)}, f32[3200,1600]{0,1:T(8,128)}), (f32[800,4800]{1,0:T(8,128)}, f32[800,1600]{1,0:T(8,128)}, f32[800,6400]{1,0:T(8,128)}, ...) | async-done | bytes 61440016 | tf_op jit(solution)/shard_map/psum | solution.py:274
  3241.5 14.5 multiply_subtract_fusion.3
  3256.1 37.8 %multiply_subtract_fusion.2 = (f32[800,4800]{1,0:T(8,128)}, f32[800,4800]{1,0:T(8,128)}, f32[800,4800]{1,0:T(8,128)}) fusion(f32[800,4800]{1,0:T(8,128)} %param.21, f32[800,4800]{1,0:T(8,128)} %get-tuple-element.93, f32[800,4800]{1,0:T(8,128)} %param.26, f32[800,4800]{1,0:T(8,128)} %param.31), kind=kLoop, calls=%fused_computation.22 | loop fusion | flops 57600000 | bytes 107520000 | tf_op jit(solution)/shard_map/sub | solution.py:152
  3293.9 48.8 %multiply_subtract_fusion.1 = (f32[800,6400]{1,0:T(8,128)}, f32[800,6400]{1,0:T(8,128)}, f32[800,6400]{1,0:T(8,128)}) fusion(f32[800,6400]{1,0:T(8,128)} %param.23, f32[800,6400]{1,0:T(8,128)} %get-tuple-element.95, f32[800,6400]{1,0:T(8,128)} %param.28, f32[800,6400]{1,0:T(8,128)} %param.33), kind=kLoop, calls=%fused_computation.14 | loop fusion | flops 76800000 | bytes 143360000 | tf_op jit(solution)/shard_map/sub | solution.py:152
  3342.7 49.1 %multiply_subtract_fusion = (f32[3200,1600]{0,1:T(8,128)}, f32[3200,1600]{0,1:T(8,128)}, f32[3200,1600]{0,1:T(8,128)}) fusion(f32[3200,1600]{0,1:T(8,128)} %param.24, f32[3200,1600]{0,1:T(8,128)} %get-tuple-element.96, f32[3200,1600]{0,1:T(8,128)} %param.29, f32[3200,1600]{0,1:T(8,128)} %param.34), kind=kLoop, calls=%fused_computation.12 | loop fusion | flops 76800000 | bytes 143360000 | tf_op jit(solution)/shard_map/sub | solution.py:152
  (137 shorter events, 7.5 us)
Async XLA Ops:
  7.2 198.4 %all-gather.6.cloned.1.call-start = ((), (), s32[]{:S(2)}) async-start(), calls=%async_computation.4 | async-start | bytes 23347200 | tf_op jit(solution)/shard_map/all_gather | solution.py:184
  16.6 260.5 %all-gather.8.cloned.1.call-start = ((), (), s32[]{:S(2)}) async-start(), calls=%async_computation.5 | async-start | bytes 7987200 | tf_op jit(solution)/shard_map/all_gather | solution.py:185
  21.0 500.3 %all-gather.10.cloned.1.call-start = ((), (), s32[]{:S(2)}) async-start(), calls=%async_computation.6 | async-start | bytes 30720000 | tf_op jit(solution)/shard_map/all_gather | solution.py:186
  35.2 730.1 %all-gather.12.cloned.1.call-start = ((), (), s32[]{:S(2)}) async-start(), calls=%async_computation.7 | async-start | bytes 30720000 | tf_op jit(solution)/shard_map/all_gather | solution.py:187
  48.3 7.4 copy-start.40
  48.3 8.5 copy-start.2
  48.3 947.3 %reduce-scatter.9.cloned.1.call-start = ((), (), s32[]{:S(2)}) async-start(), calls=%async_computation.9 | async-start | bytes 15974400 | tf_op jit(solution)/shard_map/reduce_scatter | solution.py:269
  56.5 163.7 %copy-start.19 = (f32[1600]{0:T(1024)}, f32[1600]{0:T(1024)S(1)}, u32[]{:S(2)}) copy-start(f32[1600]{0:T(1024)S(1)} %get-tuple-element.128) | copy-start | bytes 19204
  56.5 163.7 %copy-start.36 = (f32[1600]{0:T(1024)}, f32[1600]{0:T(1024)S(1)}, u32[]{:S(2)}) copy-start(f32[1600]{0:T(1024)S(1)} %get-tuple-element.127) | copy-start | bytes 19204
  56.5 464.8 %copy-start.34 = (f32[1600]{0:T(1024)}, f32[1600]{0:T(1024)S(1)}, u32[]{:S(2)}) copy-start(f32[1600]{0:T(1024)S(1)} %get-tuple-element.123) | copy-start | bytes 19204
  57.0 163.2 %copy-start.24 = (f32[512]{0:T(512)}, f32[512]{0:T(512)S(1)}, u32[]{:S(2)}) copy-start(f32[512]{0:T(512)S(1)} %broadcast_multiply_fusion.1) | copy-start | bytes 6148
  57.5 162.7 %copy-start.27 = (f32[512]{0:T(512)}, f32[512]{0:T(512)S(1)}, u32[]{:S(2)}) copy-start(f32[512]{0:T(512)S(1)} %fusion.26) | copy-start | bytes 6148
  57.5 162.7 %copy-start.29 = (f32[512]{0:T(512)}, f32[512]{0:T(512)S(1)}, u32[]{:S(2)}) copy-start(f32[512]{0:T(512)S(1)} %fusion.45) | copy-start | bytes 6148
  220.6 11.0 copy-start.3
  220.6 11.0 copy-start.5
  220.6 21.8 copy-start.15
  283.6 1.7 copy-start.7
  521.3 243.9 %copy-start.11 = (bf16[512,1600]{0,1:T(8,128)(2,1)S(1)}, bf16[512,1600]{0,1:T(8,128)(2,1)}, u32[]{:S(2)}) copy-start(bf16[512,1600]{0,1:T(8,128)(2,1)} %param.19) | copy-start | bytes 4915204
  765.3 30.7 copy-start.8
  817.2 1.7 copy-start
  817.2 4.2 copy-start.41
  817.3 10.0 copy-start.31
  827.3 469.4 %reduce-scatter.7.cloned.1.call-start = ((), (), s32[]{:S(2)}) async-start(), calls=%async_computation.8 | async-start | bytes 46694400 | tf_op jit(solution)/shard_map/reduce_scatter | solution.py:268
  833.5 17.4 copy-start.14
  850.9 22.8 copy-start.6
  873.7 10.1 copy-start.4
  891.0 14.6 copy-start.20
  891.0 14.6 copy-start.25
  891.0 14.6 copy-start.30
  891.0 14.6 copy-start.37
  923.0 825.2 %reduce-scatter.11.cloned.1.call-start = ((), (), s32[]{:S(2)}) async-start(), calls=%async_computation.10 | async-start | bytes 61440000 | tf_op jit(solution)/shard_map/reduce_scatter | solution.py:271
  945.5 1254.2 %reduce-scatter.13.cloned.1.call-start = ((), (), s32[]{:S(2)}) async-start(), calls=%async_computation.12 | async-start | bytes 61440000
  969.5 19.2 copy-start.28
  969.5 1254.0 %all-reduce.6.cloned.1.call-start = ((), (), s32[]{:S(2)}) async-start(), calls=%async_computation.11 | async-start | bytes 155648
  969.5 20.7 copy-start.13
  988.6 3.1 copy-start.1
  988.6 3.1 copy-start.12
  988.7 3.1 copy-start.32
  991.8 3.0 copy-start.23
  991.8 3.0 copy-start.26
  991.8 3.0 copy-start.38
  991.8 2.9 copy-start.39
  995.5 2246.0 %all-reduce.8.cloned.1.call-start = ((), (), s32[]{:S(2)}) async-start(), calls=%async_computation.13 | async-start | bytes 123699200 | tf_op jit(solution)/shard_map/psum | solution.py:274
  2199.7 1.9 copy-start.9
  2199.7 1.9 copy-start.33
  2201.6 87.3 %copy-start.18 = (f32[9600]{0:T(1024)S(1)}, f32[9600]{0:T(1024)}, u32[]{:S(2)}) copy-start(f32[9600]{0:T(1024)} %param.25) | copy-start | bytes 115204
  2201.6 87.3 %copy-start.21 = (f32[9600]{0:T(1024)S(1)}, f32[9600]{0:T(1024)}, u32[]{:S(2)}) copy-start(f32[9600]{0:T(1024)} %param.30) | copy-start | bytes 115204
  2201.6 87.3 %copy-start.22 = (f32[9600]{0:T(1024)S(1)}, f32[9600]{0:T(1024)}, u32[]{:S(2)}) copy-start(f32[9600]{0:T(1024)} %param.35) | copy-start | bytes 115204
  (5 other events, 5.0 us)
Sparse Core Ops, SparseCore 0:
  16.8 188.7 all-gather.5
  207.7 69.4 all-gather.7
  279.3 241.9 all-gather.9
  523.3 241.8 all-gather.11
  827.4 123.6 reduce-scatter.8
  953.2 343.3 reduce-scatter.6
  1299.1 449.0 reduce-scatter.10
  1750.6 449.0 reduce-scatter.12
  2202.6 20.8 all-reduce.5
  2229.0 1012.4 all-reduce.7
where the time goes:
time: 3400 us
  waiting for transfers between devices  2780 us (82%)
  matrix products  282 us (8%)
  other arithmetic  235 us (7%)
  blocking collectives  70.8 us (2%)
    psum x1, waiting for transfers between devices, local(): lax.psum((shares[0], shares[1], shares[2], shares[3], shares[4]), 'dp')  952 us
    unnamed x12, waiting for transfers between devices  452 us
    reduce_scatter x1, waiting for transfers between devices, local(): lax.psum_scatter(grad_down, 'shard', scatter_dimension=0, tiled=True)  452 us
    reduce_scatter x1, waiting for transfers between devices, local(): lax.psum_scatter(grad_qkv_w, 'shard', scatter_dimension=0, tiled=True)  301 us
    all_gather x1, waiting for transfers between devices, local(): lax.all_gather(lowered[2], 'shard', axis=0, tiled=True)  236 us
    all_gather x1, waiting for transfers between devices, local(): lax.all_gather(lowered[3], 'shard', axis=0, tiled=True)  222 us
    sub x5, other arithmetic, adamw_step(): master - step_rate * (corrected_m / (jnp.sqrt(corrected_v) + ADAM_EPS) +...  151 us
    all_gather x1, waiting for transfers between devices, local(): lax.all_gather(lowered[0], 'shard', axis=0, tiled=True)  148 us
  transfers between devices with their start and end apart: 10, of which 9 were waited for; matrix products, arithmetic and copies ran while one was open for 9% of the time, Pallas kernels for 0%

commit v1 on v0

v1 whole, which is shorter than its diff:
```python
import functools

import jax
import jax.numpy as jnp
from jax import lax
from jax.experimental import pallas as pl
from jax.experimental.pallas import tpu as pltpu
from jax.sharding import PartitionSpec as P

HD = 64
BLK = 128
STEP = 10


NEG_FILL = -1e30
NORM_EPS = 1e-05
GELU_SCALE = 0.7978845608028654
GELU_CUBE = 0.044715
BETA_ONE = 0.9
BETA_TWO = 0.999
LEARN_RATE = 0.06
VECTOR_RATE = 0.25
ADAM_EPS = 1e-08
WEIGHT_DECAY = 0.1

BF16 = jnp.bfloat16
F32 = jnp.float32
VMEM_LIMIT = 44 * 1024 * 1024
TILE = 256
ISSUE = 1.0
LATENCY = 3.0
HOLD = 20.17
CAP = 5
ROWS = 256

NUDGES = (
    0, 0, -33.3, -4.1, -13.2, 3.2, -5.9, -16.2, 24, -9.4, 0.6, -6.3, 9.9, -2.6, -3, -2.6,
    0, 0, 4.4, -3.2, 19.6, -3.9, 18, 27.3, 0, 5.3, 21.8, -13.9, -12, 17.4, 0, -8.2,
    5.6, 0, 0.2, 11, 0, 0.8, -11, -0.3, 6.1, -13, 21.4, 18.2, 0, 29.5, -0.5, -34.4,
    19, 14.4, -0.3, -0.6, -7.6, 0, 6.8, 5.4, 39, 0, -8.4, -2.7, 4.5, 0, 34.6, 0,
    -7.2, 4.3, -2.5, -2, 0, -45.7, -22.9, 10.9, 0, -1, -5.3, 0, -19.9, 14.6, -28.3, -19.2,
    -18.1, 0, -3.6, 7.5, 54.8, 6, -51.4, -26.3, -4.4, 20, 7.5, 0, 0, 0, 2.3, 0.7,
    -0.8, -1.2, 3.3, 4.6, 5.1, 0, 6.8, 19.6, -6.2, 8.6, 30.8, -28.3, -21.1, -2.1, 1.3, -36.9,
    -14, -2.4, 0, -0.3, 2.5, -0.9, 2.1, 0, 5.6, -3.9, -11.7, 6.9, 2.5, 54.5, 17.9, -1.2,
    -15, -25.2, 0.2, 0, 28.8, 6.2, -21.8, 0,
)

AXES = ("dp", "shard")
BIT_HALF = 1
BIT_CORE = 2
BIT_Y = 4
BIT_Z = 8
BIT_REST = 16


class Task:
    def __init__(self, name, kind, rank, cost, needs, run):
        self.name = name
        self.kind = kind
        self.rank = rank
        self.cost = cost
        self.needs = needs
        self.run = run
        self.value = None
        self.end = None


class Plan:
    def __init__(self):
        self.tasks = []

    def core(self, name, rank, cost, needs, run):
        task = Task(name, "core", rank, cost, needs, run)
        self.tasks.append(task)
        return task

    def link(self, name, rank, cost, needs, run):
        task = Task(name, "link", rank, cost, needs, run)
        self.tasks.append(task)
        return task

    def order(self):
        waiting = list(self.tasks)
        active = []
        flying = []
        steps = []
        now = 0.0

        def advance(until):
            nonlocal now
            while until is None or now < until:
                users = {}
                for task in active:
                    for axis, left in task.left.items():
                        if left > 1e-6:
                            users[axis] = users.get(axis, 0) + 1
                step = min(
                    [1e9 if until is None else until - now]
                    + [
                        left * users[axis]
                        for task in active
                        for axis, left in task.left.items()
                        if left > 1e-6
                    ]
                )
                now += step
                ended = False
                for task in list(active):
                    for axis, left in task.left.items():
                        if left > 1e-6:
                            task.left[axis] = left - step / users[axis]
                    if max(task.left.values()) <= 1e-6:
                        active.remove(task)
                        task.end = now
                        ended = True
                if until is None and ended:
                    return

        def done(task):
            return all(
                need.end is not None and need.end <= now and need not in flying
                for need in task.needs
            )

        while waiting:
            landed = [t for t in flying if t.end is not None and t.end + LATENCY <= now]
            for task in landed:
                flying.remove(task)
            queued = sorted((t for t in waiting if t.kind == "link" and done(t)), key=lambda t: t.rank)
            links = []
            for task in queued:
                if len(flying) == CAP or any(
                    sum(other.left.get(axis, 0.0) for other in active) > HOLD
                    for axis in task.cost
                    if axis != BIT_CORE
                ):
                    continue
                links.append(task)
                task.left = dict(task.cost)
                active.append(task)
                flying.append(task)
                waiting.remove(task)
                advance(now + ISSUE)
            cores = sorted((t for t in waiting if t.kind == "core" and done(t)), key=lambda t: t.rank)
            if cores:
                task = cores[0]
                waiting.remove(task)
                steps.append((landed, links, task))
                advance(now + task.cost)
                task.end = now
                continue
            if links or landed:
                steps.append((landed, links, None))
            if not any(t.end is not None for t in flying):
                advance(None)
            else:
                advance(now + 0.5)
        self.length = now
        return steps

    def trace(self):
        for task, nudge in zip(self.tasks, NUDGES):
            task.rank += nudge
        token = None
        for landed, links, task in self.order():
            group = links + ([task] if task is not None else [])
            arrived, token = lax.optimization_barrier(([t.value for t in landed], token))
            for member, value in zip(landed, arrived):
                member.value = value
            needed = [[need.value for need in member.needs] for member in group]
            needed, arrived, token = lax.optimization_barrier((needed, arrived, token))
            for member, value in zip(landed, arrived):
                member.value = value
            for member, values in zip(group, needed):
                with jax.named_scope(member.name):
                    member.value = member.run(*values)
            if task is not None:
                token = min(jax.tree.leaves(task.value), key=lambda leaf: leaf.size)


def layout(row_lengths, slot_count, block_size):
    blocks_used = (row_lengths + block_size - 1) // block_size
    starts = (jnp.cumsum(blocks_used) - blocks_used) * block_size
    position = jnp.arange(slot_count, dtype=jnp.int32)[:, None]
    inside = (position >= starts[None, :]) & (position < (starts + row_lengths)[None, :])
    labels = jnp.arange(row_lengths.shape[0], dtype=jnp.int32) + 1
    segment = jnp.sum(jnp.where(inside, labels[None, :], 0), axis=1) - 1
    return segment


def normalize(values):
    center = values - jnp.mean(values, axis=-1, keepdims=True)
    spread = jnp.mean(center * center, axis=-1, keepdims=True)
    inverse = lax.rsqrt(spread + NORM_EPS)
    return center * inverse, inverse


def normalize_back(grad, normal, inverse, gain_vec):
    scaled = grad * gain_vec
    mean_scaled = jnp.mean(scaled, axis=-1, keepdims=True)
    mean_cross = jnp.mean(scaled * normal, axis=-1, keepdims=True)
    return inverse * (scaled - mean_scaled - normal * mean_cross)


def column_sum(values):
    return jnp.sum(values, axis=0, keepdims=True)


def tiles(width, body, size=TILE):
    for start in range(0, width, size):
        body(slice(start, min(start + size, width)))


def dot_tile(x, w):
    return lax.dot_general(x, w, (((1,), (0,)), ((), ())), preferred_element_type=F32)


def dot_tile_t(x, w):
    return lax.dot_general(x, w, (((1,), (1,)), ((), ())), preferred_element_type=F32)


def params():
    return pltpu.CompilerParams(vmem_limit_bytes=VMEM_LIMIT)


def whole_block(shape):
    return pl.BlockSpec(shape, lambda *_: (0,) * len(shape))


def lead_block(shape, first=0):
    return pl.BlockSpec((1,) + shape, lambda j: (j + first,) + (0,) * len(shape))


def little():
    return pl.CostEstimate(flops=1, bytes_accessed=1, transcendentals=0)


class Weights:
    COUNT = 10

    def __init__(self, by_rows, spot, own, pieces):
        self.by_rows = by_rows
        self.operands = [spot, own] + list(pieces)
        self.width = own.shape[-1]

    def specs(self):
        return [pl.BlockSpec(memory_space=pltpu.SMEM)] + [pl.BlockSpec(memory_space=pl.ANY)] * 9

    def scratch(self):
        return [
            pltpu.VMEM((2, self.width, self.width), BF16),
            pltpu.SemaphoreType.DMA((2,)),
        ]


def start_block(by_rows, refs, buffer, sems, block, slot):
    spot, own, pieces = refs[0], refs[1], refs[2:]
    half, core, high, low = (spot[i] for i in range(4))
    width = buffer.shape[2]
    quarter = width // 4
    group, bit = block >> 1, block & 1

    def copy(source, start, size):
        rows = pl.ds(pl.multiple_of(start, 16), size)
        pltpu.make_async_copy(source, buffer.at[slot, rows], sems.at[slot]).start()

    if by_rows:
        copy(own.at[block], half * (2 * quarter), 2 * quarter)
        near = group == core
        for is_near in (True, False):
            outer, inner = (high, low) if is_near else (low, high)
            for flip in range(2):

                @pl.when((near == is_near) & ((bit ^ outer) == flip))
                def _(is_near=is_near, inner=inner, flip=flip):
                    for k in range(2):
                        start = ((1 - half) * 2 + (inner ^ k)) * quarter
                        copy(pieces[2 * (2 * flip + k) + (0 if is_near else 1)], start, quarter)

    else:

        @pl.when(group == half)
        def _():
            copy(own.at[bit], 0, width)

        for is_near in (True, False):
            outer, inner = (high, low) if is_near else (low, high)

            @pl.when((group != half) & ((bit == core) == is_near))
            def _(is_near=is_near, outer=outer, inner=inner):
                for flip in range(2):
                    for k in range(2):
                        start = ((outer ^ flip) * 2 + (inner ^ k)) * quarter
                        copy(pieces[2 * (2 * flip + k) + (0 if is_near else 1)], start, quarter)


def stream_block(by_rows, refs, buffer, sems, first):
    step = pl.program_id(0)
    slot = step & 1

    @pl.when(step == 0)
    def _():
        start_block(by_rows, refs, buffer, sems, step + first, slot)

    @pl.when(step + 1 < pl.num_programs(0))
    def _():
        start_block(by_rows, refs, buffer, sems, step + first + 1, 1 - slot)

    pltpu.make_async_copy(buffer.at[slot], buffer.at[slot], sems.at[slot]).wait()
    return slot


def norm_one_kernel(input_ref, gain_ref, shift_ref, normed_ref, rows_ref):
    for start in range(0, input_ref.shape[1], 128):
        part = slice(start, start + 128)
        rows = input_ref[:, part].astype(F32).T
        normal, _ = normalize(rows)
        normed_ref[part, :] = (normal * gain_ref[...] + shift_ref[...]).astype(BF16)
        rows_ref[part, :] = rows.astype(BF16)


def norm_one(inputs_t, gain, shift):
    width, rows = inputs_t.shape
    full = whole_block((rows, width))
    line = whole_block((1, width))
    shape = jax.ShapeDtypeStruct((rows, width), BF16)
    return pl.pallas_call(
        norm_one_kernel,
        in_specs=[whole_block((width, rows)), line, line],
        out_specs=[full, full],
        out_shape=[shape, shape],
        grid=(1,),
        compiler_params=params(),
        cost_estimate=little(),
        name="norm_one",
    )(inputs_t, gain, shift)


def mask_grad_kernel(grad_ref, live_ref, low_ref, sum_ref):
    sum_ref[...] = jnp.zeros_like(sum_ref)
    for start in range(0, grad_ref.shape[1], 128):
        part = slice(start, start + 128)
        rows = jnp.where(live_ref[:, part] > 0, grad_ref[:, part].astype(F32), 0.0).T
        low_ref[part, :] = rows.astype(BF16)
        sum_ref[...] += column_sum(rows)


def mask_grad(cotangent_t, live):
    width, rows = cotangent_t.shape
    return pl.pallas_call(
        mask_grad_kernel,
        in_specs=[whole_block((width, rows)), whole_block((1, rows))],
        out_specs=[whole_block((rows, width)), whole_block((1, width))],
        out_shape=[
            jax.ShapeDtypeStruct((rows, width), BF16),
            jax.ShapeDtypeStruct((1, width), F32),
        ],
        grid=(1,),
        compiler_params=params(),
        cost_estimate=little(),
        name="mask",
    )(cotangent_t, live)


def blocks_kernel(counts, *refs):
    ins = refs[: len(counts)]
    outs = refs[len(counts) :]
    number = 0
    for ref, count in zip(ins, counts):
        width = ref.shape[1] // count
        for j in range(count):
            outs[0][number] = ref[:, j * width : (j + 1) * width].astype(BF16)
            number += 1


def column_blocks(arrays, counts, step_rows):
    rows = arrays[0].shape[0]
    width = arrays[0].shape[1] // counts[0]
    blocks = sum(counts)
    return pl.pallas_call(
        functools.partial(blocks_kernel, counts),
        grid=(rows // step_rows,),
        in_specs=[pl.BlockSpec((step_rows, a.shape[1]), lambda i: (i, 0)) for a in arrays],
        out_specs=pl.BlockSpec((blocks, step_rows, width), lambda i: (0, i, 0)),
        out_shape=jax.ShapeDtypeStruct((blocks, rows, width), BF16),
        compiler_params=params(),
        cost_estimate=little(),
        name="cast",
    )(*arrays)


def weighted(kernel, weights, first, **call):
    inner = call.pop("operands")
    scratch = call.pop("scratch_shapes", [])
    specs = call.pop("in_specs")
    outs = call["out_shape"]
    out_count = len(outs) if isinstance(outs, list) else 1

    def body(*refs):
        weight_refs = refs[: Weights.COUNT]
        rest = refs[Weights.COUNT : Weights.COUNT + len(inner) + out_count]
        more = refs[Weights.COUNT + len(inner) + out_count :]
        buffer, sems = more[:2]
        slot = stream_block(weights.by_rows, weight_refs, buffer, sems, first)
        kernel(buffer, slot, *rest, *more[2:])

    return pl.pallas_call(
        body,
        in_specs=weights.specs() + specs,
        scratch_shapes=weights.scratch() + scratch,
        compiler_params=params(),
        cost_estimate=little(),
        **call,
    )(*weights.operands, *inner)


def project_kernel(w_ref, slot, x_ref, bias_ref, out_ref):
    def body(cols):
        total = dot_tile(x_ref[...], w_ref[slot, :, cols]) + bias_ref[0, :, cols]
        out_ref[0, :, cols] = total.astype(BF16)

    tiles(w_ref.shape[2], body, 512)


def project(normed, weights, bias):
    rows, width = normed.shape
    return weighted(
        project_kernel,
        weights,
        0,
        operands=[normed, bias],
        grid=(3,),
        in_specs=[whole_block((rows, width)), lead_block((1, width))],
        out_specs=lead_block((rows, width)),
        out_shape=jax.ShapeDtypeStruct((3, rows, width), BF16),
        name="project",
    )


def row_parts(rows, body):
    for start in range(0, rows, 128):
        body(slice(start, start + 128))


def out_kernel(
    w_ref, slot, x_ref, input_ref, bias_ref, gain_ref, shift_ref, residual_ref, normed_ref
):
    def body(cols):
        total = dot_tile(x_ref[...], w_ref[slot, :, cols]) + bias_ref[:, cols]
        residual_ref[:, cols] = input_ref[:, cols].astype(F32) + total

    tiles(w_ref.shape[2], body)

    def finish(part):
        normal, _ = normalize(residual_ref[part, :])
        normed_ref[part, :] = (normal * gain_ref[...] + shift_ref[...]).astype(BF16)

    row_parts(x_ref.shape[0], finish)


def out_and_norm(attended, weights, inputs, bias, gain, shift):
    rows, width = attended.shape
    full = whole_block((rows, width))
    line = whole_block((1, width))
    return weighted(
        out_kernel,
        weights,
        3,
        operands=[attended, inputs, bias, gain, shift],
        grid=(1,),
        in_specs=[full, full, line, line, line],
        out_specs=[full, full],
        out_shape=[
            jax.ShapeDtypeStruct((rows, width), F32),
            jax.ShapeDtypeStruct((rows, width), BF16),
        ],
        name="out",
    )


def up_kernel(w_ref, slot, x_ref, bias_ref, act_ref, slope_ref):
    def body(cols):
        pre = dot_tile(x_ref[...], w_ref[slot, :, cols]) + bias_ref[0, :, cols]
        square = pre * pre
        bend = jnp.tanh(GELU_SCALE * pre * (1.0 + GELU_CUBE * square))
        half = 0.5 + 0.5 * bend
        act_ref[0, :, cols] = (pre * half).astype(BF16)
        inner = GELU_SCALE + (3.0 * GELU_CUBE * GELU_SCALE) * square
        slope_ref[0, :, cols] = half + (0.5 * pre) * (1.0 - bend * bend) * inner

    tiles(w_ref.shape[2], body, 512)


def up_and_gelu(normed, weights, bias):
    rows, width = normed.shape
    return weighted(
        up_kernel,
        weights,
        0,
        operands=[normed, bias],
        grid=(4,),
        in_specs=[whole_block((rows, width)), lead_block((1, width))],
        out_specs=[lead_block((rows, width)), lead_block((rows, width))],
        out_shape=[
            jax.ShapeDtypeStruct((4, rows, width), BF16),
            jax.ShapeDtypeStruct((4, rows, width), F32),
        ],
        name="up",
    )


def grad_pre_kernel(w_ref, slot, x_ref, slope_ref, out_ref, sum_ref):
    def body(cols):
        total = dot_tile(x_ref[...], w_ref[slot, :, cols]) * slope_ref[0, :, cols]
        low = total.astype(BF16)
        out_ref[0, :, cols] = low
        sum_ref[0, :, cols] = column_sum(low.astype(F32))

    tiles(w_ref.shape[2], body)


def grad_pre_act(grad_low, weights, slope):
    rows, width = grad_low.shape
    return weighted(
        grad_pre_kernel,
        weights,
        0,
        operands=[grad_low, slope],
        grid=(4,),
        in_specs=[whole_block((rows, width)), lead_block((rows, width))],
        out_specs=[lead_block((rows, width)), lead_block((1, width))],
        out_shape=[
            jax.ShapeDtypeStruct((4, rows, width), BF16),
            jax.ShapeDtypeStruct((4, 1, width), F32),
        ],
        name="g_pre",
    )


def add_product_t(w_ref, slot, x_ref, total_ref, size=TILE):
    later = pl.program_id(0) > 0

    def body(cols):
        part = dot_tile_t(x_ref[0], w_ref[slot, cols, :])
        total_ref[:, cols] = jnp.where(later, total_ref[:, cols], 0.0) + part

    tiles(w_ref.shape[1], body, size)


def last_step():
    return pl.program_id(0) == pl.num_programs(0) - 1


def norm_two_back_kernel(
    w_ref, slot, x_ref, residual_ref, grad_ref, gain_ref, out_ref, low_ref, sums_ref, total_ref
):
    add_product_t(w_ref, slot, x_ref, total_ref, 512)

    @pl.when(last_step())
    def _():
        sums_ref[...] = jnp.zeros_like(sums_ref)

        def body(part):
            normal, inverse = normalize(residual_ref[part, :])
            grad = total_ref[part, :]
            back = normalize_back(grad, normal, inverse, gain_ref[...])
            back = grad_ref[part, :].astype(F32) + back
            low = back.astype(BF16)
            out_ref[part, :] = back
            low_ref[part, :] = low
            sums_ref[0:1, :] += column_sum(grad * normal)
            sums_ref[1:2, :] += column_sum(grad)
            sums_ref[2:3, :] += column_sum(low.astype(F32))

        row_parts(total_ref.shape[0], body)


def norm_two_back(grad_pre, weights, residual, grad_low, gain):
    blocks, rows, width = grad_pre.shape
    full = whole_block((rows, width))
    return weighted(
        norm_two_back_kernel,
        weights,
        0,
        operands=[grad_pre, residual, grad_low, gain],
        grid=(blocks,),
        in_specs=[lead_block((rows, width)), full, full, whole_block((1, width))],
        out_specs=[full, full, whole_block((8, width))],
        out_shape=[
            jax.ShapeDtypeStruct((rows, width), F32),
            jax.ShapeDtypeStruct((rows, width), BF16),
            jax.ShapeDtypeStruct((8, width), F32),
        ],
        scratch_shapes=[pltpu.VMEM((rows, width), F32)],
        name="n2_b",
    )


def norm_one_back_kernel(
    w_ref, slot, x_ref, input_ref, grad_ref, gain_ref, out_ref, sums_ref, total_ref
):
    add_product_t(w_ref, slot, x_ref, total_ref)

    @pl.when(last_step())
    def _():
        sums_ref[...] = jnp.zeros_like(sums_ref)

        def body(part):
            normal, inverse = normalize(input_ref[part, :].astype(F32))
            grad = total_ref[part, :]
            back = normalize_back(grad, normal, inverse, gain_ref[...])
            out_ref[:, part] = (grad_ref[part, :] + back).T.astype(BF16)
            sums_ref[0:1, :] += column_sum(grad * normal)
            sums_ref[1:2, :] += column_sum(grad)

        row_parts(total_ref.shape[0], body)


def norm_one_back(grad_parts, weights, inputs, grad_residual, gain):
    blocks, rows, width = grad_parts.shape
    full = whole_block((rows, width))
    return weighted(
        norm_one_back_kernel,
        weights,
        0,
        operands=[grad_parts, inputs, grad_residual, gain],
        grid=(blocks,),
        in_specs=[lead_block((rows, width)), full, full, whole_block((1, width))],
        out_specs=[whole_block((width, rows)), whole_block((8, width))],
        out_shape=[
            jax.ShapeDtypeStruct((width, rows), BF16),
            jax.ShapeDtypeStruct((8, width), F32),
        ],
        scratch_shapes=[pltpu.VMEM((rows, width), F32)],
        name="n1_b",
    )


def layer_out_kernel(w_ref, slot, x_ref, residual_ref, live_ref, bias_ref, out_ref, total_ref):
    add_product_t(w_ref, slot, x_ref, total_ref, 1600)

    @pl.when(last_step())
    def _():
        def body(part):
            result = residual_ref[part, :] + (total_ref[part, :] + bias_ref[...])
            out_ref[:, part] = jnp.where(live_ref[:, part] > 0, result.T, 0.0).astype(BF16)

        row_parts(total_ref.shape[0], body)


def layer_out(activated, weights, residual, live, bias):
    blocks, rows, width = activated.shape
    full = whole_block((rows, width))
    return weighted(
        layer_out_kernel,
        weights,
        0,
        operands=[activated, residual, live, bias],
        grid=(blocks,),
        in_specs=[
            lead_block((rows, width)),
            full,
            whole_block((1, rows)),
            whole_block((1, width)),
        ],
        out_specs=whole_block((width, rows)),
        out_shape=jax.ShapeDtypeStruct((width, rows), BF16),
        scratch_shapes=[pltpu.VMEM((rows, width), F32)],
        name="layer",
    )


def grad_attended_kernel(w_ref, slot, x_ref, out_ref):
    def body(cols):
        out_ref[:, cols] = dot_tile_t(x_ref[...], w_ref[slot, cols, :]).astype(BF16)

    tiles(w_ref.shape[1], body)


def grad_attended_of(grad_branch, weights):
    rows, width = grad_branch.shape
    full = whole_block((rows, width))
    return weighted(
        grad_attended_kernel,
        weights,
        3,
        operands=[grad_branch],
        grid=(1,),
        in_specs=[full],
        out_specs=full,
        out_shape=jax.ShapeDtypeStruct((rows, width), BF16),
        name="g_att",
    )


def outer_kernel(extra, places_ref, left_ref, right_ref, *refs):
    total = lax.dot_general(
        left_ref[0], right_ref[0], (((0,), (0,)), ((), ())), preferred_element_type=F32
    )
    if extra:
        total = total + refs[0][0].astype(F32)
    refs[-1][0] = total.astype(BF16)


def outer_products(left, right, places, other=None):
    _, rows, width = left.shape
    count = places.shape[0] // 2
    part = pl.BlockSpec((1, TILE, width), lambda b, i, at: (b, i, 0))
    extra = [] if other is None else [other]
    return pl.pallas_call(
        functools.partial(outer_kernel, bool(extra)),
        grid_spec=pltpu.PrefetchScalarGridSpec(
            num_scalar_prefetch=1,
            grid=(count, pl.cdiv(width, TILE)),
            in_specs=[
                pl.BlockSpec((1, rows, TILE), lambda b, i, at: (at[2 * b], 0, i)),
                pl.BlockSpec((1, rows, width), lambda b, i, at: (at[2 * b + 1], 0, 0)),
            ]
            + [part] * len(extra),
            out_specs=part,
        ),
        out_shape=jax.ShapeDtypeStruct((count, width, width), BF16),
        compiler_params=params(),
        cost_estimate=little(),
        name="outer",
    )(places, left, right, *extra)


def head_lanes(ref, index, head, valid, lane):
    mine = valid & ((lane < HD) if head == 0 else (lane >= HD))
    return jnp.where(mine, ref[index], jnp.zeros((), BF16))


def attend_kernel(width, qkv_ref, fill_ref, out_ref, lse_ref):
    pair = pl.program_id(0)
    rows = qkv_ref.shape[1]
    lane = lax.broadcasted_iota(jnp.int32, (rows, 2 * HD), 1)
    valid = lane + pair * (2 * HD) < width
    totals = [None] * (rows // ROWS)
    column = lax.broadcasted_iota(jnp.int32, (ROWS, lse_ref.shape[1]), 1)
    for head in range(2):
        query = head_lanes(qkv_ref, 0, head, valid, lane) * 0.125
        key = head_lanes(qkv_ref, 1, head, valid, lane)
        value = head_lanes(qkv_ref, 2, head, valid, lane)
        for number in range(rows // ROWS):
            part = slice(number * ROWS, (number + 1) * ROWS)
            seen = slice(0, (number + 1) * ROWS)
            scores = dot_tile_t(query[part], key[seen]) + fill_ref[part, seen]
            row_max = jnp.max(scores, axis=-1, keepdims=True)
            exponent = jnp.exp(scores - row_max)
            total = jnp.sum(exponent, axis=-1, keepdims=True)
            probs = (exponent * (1.0 / total)).astype(BF16)
            result = dot_tile(probs, value[seen])
            totals[number] = result if head == 0 else totals[number] + result
            lse = row_max + jnp.log(total)
            lse_ref[part, :] = jnp.where(column == pair * 2 + head, lse, lse_ref[part, :])
    for number in range(rows // ROWS):
        out_ref[number * ROWS : (number + 1) * ROWS, :] = totals[number].astype(BF16)


def attend_forward(projected, fill):
    _, rows, width = projected.shape
    pairs = pl.cdiv(width, 2 * HD)
    return pl.pallas_call(
        functools.partial(attend_kernel, width),
        grid=(pairs,),
        in_specs=[
            pl.BlockSpec((3, rows, 2 * HD), lambda h: (0, 0, h)),
            whole_block((rows, rows)),
        ],
        out_specs=[
            pl.BlockSpec((rows, 2 * HD), lambda h: (0, h)),
            whole_block((rows, 128)),
        ],
        out_shape=[
            jax.ShapeDtypeStruct((rows, width), BF16),
            jax.ShapeDtypeStruct((rows, 128), F32),
        ],
        compiler_params=params(),
        cost_estimate=little(),
        name="attend",
    )(projected, fill)


def attend_back_kernel(width, first, qkv_ref, grad_ref, fill_ref, lse_ref, *refs):
    out_ref, query_ref, key_ref, value_ref = refs[-4:]
    pair = pl.program_id(0) + first
    rows = qkv_ref.shape[1]
    lane = lax.broadcasted_iota(jnp.int32, (rows, 2 * HD), 1)
    valid = lane + pair * (2 * HD) < width
    column = lax.broadcasted_iota(jnp.int32, (ROWS, lse_ref.shape[1]), 1)
    query_ref[...] = jnp.zeros_like(query_ref)
    key_ref[...] = jnp.zeros_like(key_ref)
    value_ref[...] = jnp.zeros_like(value_ref)
    contract = (((0,), (0,)), ((), ()))
    for head in range(2):
        query = head_lanes(qkv_ref, 0, head, valid, lane) * 0.125
        key = head_lanes(qkv_ref, 1, head, valid, lane)
        value = head_lanes(qkv_ref, 2, head, valid, lane)
        grad_mine = valid & ((lane < HD) if head == 0 else (lane >= HD))
        grad = jnp.where(grad_mine, grad_ref[...], jnp.zeros((), BF16))
        for number in range(rows // ROWS):
            part = slice(number * ROWS, (number + 1) * ROWS)
            seen = slice(0, (number + 1) * ROWS)
            lse = jnp.sum(
                jnp.where(column == pair * 2 + head, lse_ref[part, :], 0.0), axis=-1, keepdims=True
            )
            scores = dot_tile_t(query[part], key[seen]) + fill_ref[part, seen]
            probs = jnp.exp(scores - lse)
            grad_probs = dot_tile_t(grad[part], value[seen])
            inner = jnp.sum(grad_probs * probs, axis=-1, keepdims=True)
            grad_scores = (probs * (grad_probs - inner)).astype(BF16)
            query_ref[part, :] += dot_tile(grad_scores, key[seen])
            key_ref[seen, :] += lax.dot_general(
                grad_scores, query[part], contract, preferred_element_type=F32
            )
            value_ref[seen, :] += lax.dot_general(
                probs.astype(BF16), grad[part], contract, preferred_element_type=F32
            )
    out_ref[0] = (query_ref[...] * 0.125).astype(BF16)
    out_ref[1] = key_ref[...].astype(BF16)
    out_ref[2] = value_ref[...].astype(BF16)


def attend_backward(projected, grad_attended, fill, lse, first, count, earlier=None):
    _, rows, width = projected.shape
    three = pl.BlockSpec((3, rows, 2 * HD), lambda h: (0, 0, h + first))
    kept = [] if earlier is None else [earlier]
    return pl.pallas_call(
        functools.partial(attend_back_kernel, width, first),
        grid=(count,),
        in_specs=[
            three,
            pl.BlockSpec((rows, 2 * HD), lambda h: (0, h + first)),
            whole_block((rows, rows)),
            whole_block((rows, 128)),
        ]
        + [pl.BlockSpec(memory_space=pl.ANY)] * len(kept),
        out_specs=three,
        out_shape=jax.ShapeDtypeStruct((3, rows, width), BF16),
        scratch_shapes=[pltpu.VMEM((rows, 2 * HD), F32)] * 3,
        input_output_aliases={4: 0} if kept else {},
        compiler_params=params(),
        cost_estimate=little(),
        name="attend_b",
    )(projected, grad_attended, fill, lse, *kept)


def adamw_step(master, gradient, momentum, variance, decay_rate, step_rate):
    momentum_new = BETA_ONE * momentum + (1.0 - BETA_ONE) * gradient
    variance_new = BETA_TWO * variance + (1.0 - BETA_TWO) * gradient * gradient
    corrected_m = momentum_new / (1.0 - BETA_ONE**STEP)
    corrected_v = variance_new / (1.0 - BETA_TWO**STEP)
    updated = master - step_rate * (
        corrected_m / (jnp.sqrt(corrected_v) + ADAM_EPS) + decay_rate * master
    )
    return (updated, momentum_new, variance_new)


def adamw_kernel(picks, core_ref, w_ref, m_ref, v_ref, *refs):
    nw_ref, nm_ref, nv_ref = refs[-3:]
    first = core_ref[0] == 0
    blocks = []
    for number, core in picks:
        own, other = (refs[2 * number + i][0].astype(F32) for i in range(2))
        blocks.append(jnp.where(first, own, other) if core == 0 else jnp.where(first, other, own))
    gradient = blocks[0] if len(blocks) == 1 else jnp.concatenate(blocks, axis=1)
    nw_ref[...], nm_ref[...], nv_ref[...] = adamw_step(
        w_ref[...], gradient, m_ref[...], v_ref[...], WEIGHT_DECAY, LEARN_RATE
    )


def adamw_part(core, state, picks, step_rows, row_part=0, col_part=0, earlier=None):
    _, rows, width = picks[0][0][0].shape
    cols = len(picks) * width
    steps = rows // step_rows
    spec = pl.BlockSpec((step_rows, cols), lambda i: (i + row_part * steps, col_part))
    flat, grad_specs, chosen, known = [], [], [], []
    for pair, entry, from_core in picks:
        if (id(pair), entry) not in known:
            known.append((id(pair), entry))
            flat += list(pair)
            grad_specs += [
                pl.BlockSpec((1, step_rows, width), lambda i, entry=entry: (entry, i, 0))
            ] * 2
        chosen.append((known.index((id(pair), entry)), from_core))
    kept = [] if earlier is None else list(earlier)
    shape = jax.ShapeDtypeStruct(state[0].shape, F32)
    return pl.pallas_call(
        functools.partial(adamw_kernel, chosen),
        grid=(steps,),
        in_specs=[pl.BlockSpec(memory_space=pltpu.SMEM)]
        + [spec] * 3
        + grad_specs
        + [pl.BlockSpec(memory_space=pl.ANY)] * len(kept),
        out_specs=[spec] * 3,
        out_shape=[shape] * 3,
        input_output_aliases={4 + len(flat) + i: i for i in range(len(kept))},
        compiler_params=params(),
        cost_estimate=little(),
        name="adamw",
    )(core, *state, *flat, *kept)


def pick(array, index, axis=0):
    return lax.dynamic_index_in_dim(array, index, axis, keepdims=False)


def add_low(*terms):
    total = terms[0].astype(F32)
    for term in terms[1:]:
        total = total + term.astype(F32)
    return total.astype(BF16)


class Links:
    def __init__(self, plan, devices):
        self.plan = plan
        self.devices = devices
        self.half = lax.axis_index("shard")
        index = lax.axis_index("dp")
        self.core = index % 2
        self.y = (index // 2) % 2
        self.z = (index // 4) % 2

    def swap(self, name, rank, needs, prepare, size, bit, bit_one=None):
        bit_one = bit if bit_one is None else bit_one
        pairs = [(i, i ^ (bit_one if i & BIT_CORE else bit)) for i in range(self.devices)]
        cost = {}
        for each in (bit, bit_one):
            rate = 6e5 if each == BIT_CORE else 1e5
            hops = 2 if each >= BIT_REST else 1
            share = 0.5 if each == BIT_CORE else 1.0
            cost[each] = cost.get(each, 0.0) + size * 2.08 * hops * share / rate

        def run(*values):
            return lax.ppermute(prepare(*values), AXES, pairs)

        return self.plan.link(name, rank, cost, needs, run)


def same(value):
    return value


def gather_chunk(links, name, rank, send, rows, width):
    size = rows * width
    first = links.swap(name + "_x", rank, [send], same, size, BIT_HALF)
    second = links.swap(name + "_a", rank, [first], same, size, BIT_Y, BIT_Z)
    third = links.swap(name + "_b", rank, [first], same, size, BIT_Z, BIT_Y)
    fourth = links.swap(name + "_ab", rank, [second], same, size, BIT_Z, BIT_Y)
    pieces = []
    for near in (first, second, third, fourth):
        pieces.append(near)
        pieces.append(links.swap(near.name + "c", rank, [near], same, size, BIT_CORE))
    return pieces


def reduce_chunk(links, plan, name, rank, even, ready, count, rows, width, quarter):
    core = links.core
    p_bits = (BIT_Y, BIT_Z) if even else (BIT_Z, BIT_Y)
    q_bits = (p_bits[1], p_bits[0])
    at = {BIT_Y: links.y, BIT_Z: links.z}
    p = jnp.where(core == 0, at[p_bits[0]], at[p_bits[1]])
    q = jnp.where(core == 0, at[q_bits[0]], at[q_bits[1]])
    first = core == 0
    size = count * rows * width
    send_b = (1 - core, jnp.where(first, p, 1 - p))
    keep_a = (core, jnp.where(first, 1 - p, p))

    def core_task(step, cost, needs, run):
        return plan.core(name + step, rank, cost * (0.5 + 0.5 * count), needs, run)

    def swap(step, needs, prepare, size, *bits):
        return links.swap(name + step, rank, needs, prepare, size, *bits)

    cut = core_task("cut", 3.0, [ready], lambda v: (quarter(v, 1, 1 - p), quarter(v, *send_b)))
    got_a = swap("sa", [cut], lambda v: v[0], size, BIT_HALF, p_bits[1])
    got_b = swap("sb", [cut, got_a], lambda v, _: v[1], size, BIT_HALF, p_bits[1])
    sum_a = core_task("aa", 2.5, [ready, got_a], lambda v, g: add_low(quarter(v, *keep_a), g))
    got_c = swap("sc", [sum_a], same, size, p_bits[0], BIT_HALF)

    def add_three(v, g, h):
        total = add_low(quarter(v, 0, p), g, h).reshape(count, 2, rows // 2, width)
        return pick(total, 1 - q, 1), pick(total, q, 1)

    sum_b = core_task("ab", 3.5, [ready, got_b, got_c], add_three)
    got_d = swap("sd", [sum_b], lambda v: v[0], size // 2, *q_bits)
    total = core_task("ad", 1.5, [sum_b, got_d], lambda v, d: add_low(v[1], d))
    bit = BIT_REST
    while bit < links.devices:
        got = swap("se", [total], same, size // 2, bit)
        total = core_task("ae", 1.5, [total, got], add_low)
        bit *= 2
    at_q = swap("gq", [total], same, size // 2, *q_bits)
    at_p = swap("gp", [total], same, size // 2, *p_bits)
    at_pq = swap("gr", [at_q], same, size // 2, *p_bits)

    def join(a, b, c, d):
        full = jnp.zeros((count, 2, 2, rows // 2, width), BF16)
        for value, (i, j) in ((a, (p, q)), (b, (p, 1 - q)), (c, (1 - p, q)), (d, (1 - p, 1 - q))):
            zero = jnp.zeros((), jnp.int32)
            full = lax.dynamic_update_slice(full, value[:, None, None], (zero, i, j, zero, zero))
        return full.reshape(count, 2 * rows, width)

    own = core_task("j", 5.0, [total, at_q, at_p, at_pq], join)
    other = swap("gc", [own], same, 2 * size, BIT_CORE)
    return own, other


def local(devices, *arguments):
    (
        inputs,
        cotangent,
        seq_lengths,
        qkv_weight,
        out_weight,
        up_weight,
        down_weight,
        vector_params,
        qkv_momentum,
        out_momentum,
        up_momentum,
        down_momentum,
        vector_momentum,
        qkv_variance,
        out_variance,
        up_variance,
        down_variance,
        vector_variance,
    ) = arguments
    plan = Plan()
    links = Links(plan, devices)
    half, core = links.half, links.core
    core_flag = core.reshape(1)
    slot_count, width = inputs.shape
    half_rows = width // 2
    quarter_rows = width // 4
    down_t = down_weight.T

    def given(value):
        task = Task("given", "core", 0, 0.0, [], None)
        task.value = value
        task.end = 0.0
        return task

    high = jnp.where(core == 0, links.z, links.y)
    low = jnp.where(core == 0, links.y, links.z)
    block_at = core * 2 + high
    spot = jnp.stack([half, core, high, low]).astype(jnp.int32)

    def send_qkvo(qkv, out):
        start = low * quarter_rows
        rows = lax.dynamic_slice_in_dim(qkv, start, quarter_rows, 0)
        chosen = lax.dynamic_slice_in_dim(out, start, quarter_rows, 0)
        for number in range(3):
            option = rows[:, number * width : (number + 1) * width]
            chosen = jnp.where(block_at == number, option, chosen)
        return chosen.astype(BF16)

    def send_piece(own):
        return pick(own.reshape(8, quarter_rows, width), block_at * 2 + low)

    vector_low = plan.core(
        "v_low", 0, 1.0, [given(vector_params)], lambda v: v.astype(BF16).reshape(6, width)
    )
    vector_other = links.swap("v", 0, [vector_low], same, 6 * width, BIT_HALF)
    sent_qkvo = plan.core("q_cut", 1, 8.0, [given(qkv_weight), given(out_weight)], send_qkvo)
    own_up = plan.core(
        "u_own", 2, 14.2, [given(up_weight)], lambda w: column_blocks([w], [4], 80)
    )
    sent_up = plan.core("u_cut", 2, 4.0, [own_up], send_piece)
    own_down = plan.core(
        "d_own", 3.5, 14.2, [given(down_t)], lambda w: column_blocks([w], [2], 160)
    )
    sent_down = plan.core("d_cut", 3.5, 2.5, [own_down], send_piece)
    own_qkvo = plan.core(
        "q_own",
        3,
        13.0,
        [given(qkv_weight), given(out_weight)],
        lambda w, o: column_blocks([w, o], [3, 1], 80),
    )
    pieces_qkvo = gather_chunk(links, "q_g", 1, sent_qkvo, quarter_rows, width)
    pieces_up = gather_chunk(links, "u_g", 2, sent_up, quarter_rows, width)
    pieces_down = gather_chunk(links, "d_g", 3, sent_down, quarter_rows, width)
    needs_qkvo = [own_qkvo] + pieces_qkvo
    needs_up = [own_up] + pieces_up
    needs_down = [own_down] + pieces_down

    def weights_of(by_rows, values):
        return Weights(by_rows, spot, values[0], values[1:])

    def prepare(lengths, grads):
        segment = layout(lengths[0], slot_count, BLK)
        position = jnp.arange(slot_count, dtype=jnp.int32)
        allowed = (segment[:, None] == segment[None, :]) & (position[None, :] <= position[:, None])
        fill = jnp.where(allowed, 0.0, NEG_FILL)
        live = (segment >= 0).astype(F32)[None, :]
        grad_low, grad_sum = mask_grad(grads, live)
        return fill, live, grad_low, grad_sum[0]

    prepared = plan.core("prepare", 7, 5.0, [given(seq_lengths), given(cotangent.T)], prepare)

    def join_vector(own, other):
        lower = half == 0
        pair = [jnp.where(lower, own, other), jnp.where(lower, other, own)]
        return jnp.concatenate(pair).astype(F32)

    vector = plan.core("v_join", 8, 1.0, [vector_low, vector_other], join_vector)
    normed = plan.core(
        "norm_one",
        9,
        4.0,
        [given(inputs.T), vector],
        lambda rows, vec: norm_one(rows, vec[0:1], vec[1:2]),
    )

    def qkv_bias(vec):
        return jnp.stack([vec[2], jnp.zeros_like(vec[2]), vec[3]])[:, None, :]

    projected = plan.core(
        "project",
        10,
        15.5,
        [normed, vector] + needs_qkvo,
        lambda n, vec, *w: project(n[0], weights_of(True, w), qkv_bias(vec)),
    )
    attended = plan.core(
        "attend", 11, 19.0, [projected, prepared], lambda qkv, prep: attend_forward(qkv, prep[0])
    )
    residual = plan.core(
        "out",
        12,
        12.0,
        [attended, normed, vector] + needs_qkvo,
        lambda att, n, vec, *w: out_and_norm(
            att[0], weights_of(True, w), n[1], vec[4:5], vec[5:6], vec[6:7]
        ),
    )
    activated = plan.core(
        "up",
        16,
        24.0,
        [residual, vector] + needs_up,
        lambda res, vec, *w: up_and_gelu(res[1], weights_of(True, w), vec[7:11][:, None, :]),
    )

    def places(*entries):
        return jnp.stack([jnp.asarray(entry, jnp.int32) for entry in entries])

    def down_product(act, prep, at_core, got=None):
        at = places(0, 2 * (1 - half) + at_core, 0, 2 * half + at_core)
        return outer_products(prep[2][None], act[0], at, got)

    block_size = width * width
    down_sent = plan.core(
        "d_s", 20, 12.5, [activated, prepared], lambda a, p: down_product(a, p, 1 - core)
    )
    down_got = links.swap("d_c", 20, [down_sent], same, 2 * block_size, BIT_CORE)
    down_kept = plan.core(
        "d_k",
        22,
        17.0,
        [activated, prepared, down_got],
        lambda a, p, got: down_product(a, p, core, got),
    )

    def cut_piece(value, lead, sizes):
        start = [jnp.asarray(at, jnp.int32) for at in lead] + [jnp.zeros((), jnp.int32)] * 2
        piece = lax.dynamic_slice(value, start, sizes + (quarter_rows, width))
        return piece.reshape(-1, quarter_rows, width)

    def down_quarter(value, away, p):
        value = value.reshape(2, 2, 2, quarter_rows, width)
        return cut_piece(value, (1 - away, 0, p), (1, 2, 1))

    def up_quarter(value, away, p):
        value = value.reshape(2, 2, 2, quarter_rows, width)
        return cut_piece(value, (0, half ^ away, p), (2, 1, 1))

    def block_quarter(value, away, p):
        value = value.reshape(2, 2, quarter_rows, width)
        return cut_piece(value, (half ^ away, p), (1, 1))

    def reduce(name, rank, even, ready, count, quarter):
        return reduce_chunk(
            links, plan, name, rank, even, ready, count, quarter_rows, width, quarter
        )

    down_sum = reduce("d", 0.1, True, down_kept, 2, down_quarter)

    grad_pre = plan.core(
        "g_pre",
        30,
        24.0,
        [prepared, activated] + needs_down,
        lambda prep, act, *w: grad_pre_act(prep[2], weights_of(False, w), act[1]),
    )
    def up_product(res, g, at_core, got=None):
        return outer_products(res[1][None], g[0], places(0, at_core, 0, 2 + at_core), got)

    up_sent = plan.core("u_s", 31, 12.5, [residual, grad_pre], lambda r, g: up_product(r, g, 1 - core))
    up_got = links.swap("u_c", 31, [up_sent], same, 2 * block_size, BIT_CORE)
    branch = plan.core(
        "n2_b",
        32,
        28.0,
        [grad_pre, residual, prepared, vector] + needs_up,
        lambda g, res, prep, vec, *w: norm_two_back(
            g[0], weights_of(True, w), res[0], prep[2], vec[5:6]
        ),
    )
    up_kept = plan.core(
        "u_k",
        33,
        17.0,
        [residual, grad_pre, up_got],
        lambda r, g, got: up_product(r, g, core, got),
    )
    up_sum = reduce("u", 0.2, False, up_kept, 2, up_quarter)

    grad_attended = plan.core(
        "g_att",
        34,
        9.0,
        [branch] + needs_qkvo,
        lambda b, *w: grad_attended_of(b[1], weights_of(True, w)),
    )
    pairs = pl.cdiv(width, 2 * HD)
    early = pairs // 2
    back_needs = [projected, grad_attended, prepared, attended]
    grad_early = plan.core(
        "att_b",
        35,
        16.0,
        back_needs,
        lambda qkv, g, prep, att: attend_backward(qkv, g, prep[0], att[1], 0, early),
    )
    grad_parts = plan.core(
        "att_b",
        35,
        17.0,
        back_needs + [grad_early],
        lambda qkv, g, prep, att, some: attend_backward(
            qkv, g, prep[0], att[1], early, pairs - early, some
        ),
    )

    def first_product(n, att, b, parts, at_core, got=None):
        left = jnp.where(at_core == 0, n[0], att[0])
        right = jnp.where(at_core == 0, parts[0], b[1])
        return outer_products(left[None], right[None], places(0, 0), got)

    def second_product(n, att, b, parts, at_core, got=None):
        return outer_products(n[0][None], parts, places(0, 1 + at_core), got)

    attention_needs = [normed, attended, branch, grad_parts]
    attention_sums = []
    for number, product in enumerate((first_product, second_product)):
        name = "ab"[number]
        sent = plan.core(
            name + "_s",
            36 + number,
            7.5,
            attention_needs,
            lambda *v, product=product: product(*v, 1 - core),
        )
        got = links.swap(name + "_c", 36 + number, [sent], same, block_size, BIT_CORE)
        kept = plan.core(
            name + "_k",
            38 + number,
            9.0,
            attention_needs + [got],
            lambda *v, product=product: product(*v[:4], core, v[4]),
        )
        attention_sums.append(
            reduce(name, 0.3 + 0.1 * number, number == 0, kept, 1, block_quarter)
        )
    grad_input = plan.core(
        "n1_b",
        38,
        21.5,
        [grad_parts, normed, branch, vector] + needs_qkvo,
        lambda parts, n, b, vec, *w: norm_one_back(
            parts, weights_of(True, w), n[1], b[0], vec[0:1]
        ),
    )

    def vector_grads(parts, b, g, grad_in, prep):
        part_sums = jnp.sum(parts.astype(F32), axis=1)
        rows = [grad_in[1][0], grad_in[1][1], part_sums[0], part_sums[2]]
        rows += [b[2][2], b[2][0], b[2][1]]
        rows += [g[1][j, 0] for j in range(4)] + [prep[3]]
        both = jnp.stack(rows).reshape(2, 6, width)
        return pick(both, 1 - half), pick(both, half)

    vector_grad = plan.core(
        "v_grad", 39, 3.0, [grad_parts, branch, grad_pre, grad_input, prepared], vector_grads
    )
    vector_got = links.swap("v_x", 39, [vector_grad], lambda v: v[0], 12 * width, BIT_HALF)
    vector_sum = plan.core(
        "v_add", 39, 0.5, [vector_grad, vector_got], lambda v, g: v[1] + g
    )
    bit = BIT_CORE
    while bit < devices:
        vector_got = links.swap("v_dp", 39, [vector_sum], same, 12 * width, bit)
        vector_sum = plan.core("v_add", 39, 0.5, [vector_sum, vector_got], jnp.add)
        bit *= 2

    layer = plan.core(
        "layer",
        40,
        22.0,
        [activated, residual, prepared, vector] + needs_down,
        lambda act, res, prep, vec, *w: layer_out(
            act[0], weights_of(False, w), res[0], prep[1], vec[11:12]
        ),
    )

    up_state = (up_weight, up_momentum, up_variance)
    down_state = (down_t, down_momentum.T, down_variance.T)
    qkv_state = (qkv_weight, qkv_momentum, qkv_variance)
    out_state = (out_weight, out_momentum, out_variance)

    def update(name, rank, cost, state, sums, earlier, run):
        needs = [task for pair in sums for task in pair] + ([earlier] if earlier else [])

        def call(*v):
            pairs = [v[2 * i : 2 * i + 2] for i in range(len(sums))]
            picks, extra = run(pairs)
            return adamw_part(core_flag, state, picks, 80, earlier=v[-1] if earlier else None, **extra)

        return plan.core(name, rank, cost, needs, call)

    new_down = new_up = None
    for part in range(2):
        new_down = update(
            "n_d",
            50,
            28.0,
            down_state,
            [down_sum],
            new_down,
            lambda pairs, part=part: (
                [(pairs[0], part, 0), (pairs[0], part, 1)],
                dict(row_part=part),
            ),
        )
    for part in range(2):
        new_up = update(
            "n_u",
            52,
            28.5,
            up_state,
            [up_sum],
            new_up,
            lambda pairs, part=part: (
                [(pairs[0], part, 0), (pairs[0], part, 1)],
                dict(col_part=part),
            ),
        )
    new_out = update(
        "n_o", 54, 15.0, out_state, attention_sums[:1], None, lambda p: ([(p[0], 0, 1)], {})
    )
    new_qkv = update(
        "n_q",
        55,
        39.0,
        qkv_state,
        attention_sums,
        None,
        lambda p: ([(p[0], 0, 0), (p[1], 0, 0), (p[1], 0, 1)], {}),
    )
    new_vector = plan.core(
        "n_v",
        45,
        1.0,
        [vector_sum],
        lambda g: adamw_step(
            vector_params, g.reshape(-1), vector_momentum, vector_variance, 0.0, VECTOR_RATE
        ),
    )
    plan.trace()
    states = [
        (new_qkv.value[i], new_out.value[i], new_up.value[i], new_down.value[i].T, new_vector.value[i])
        for i in range(3)
    ]
    return (layer.value.T, grad_input.value[0].T) + states[0] + states[1] + states[2]


def solution(mesh):
    rows = P(("dp", "shard"), None)
    halves = P("shard", None)
    vector = P("shard")
    state = (halves, halves, halves, halves, vector)
    return jax.shard_map(
        functools.partial(local, mesh.shape["dp"] * mesh.shape["shard"]),
        mesh=mesh,
        in_specs=(rows, rows, rows) + state * 3,
        out_specs=(rows, rows) + state * 3,
        check_vma=False,
    )
```

time: 3400 us -> 911 us (0.27)
  waiting for transfers between devices: 2780 us -> 222 us
  Pallas kernels: 0 us -> 494 us
  matrix products: 282 us -> 0 us
  other arithmetic: 235 us -> 40.9 us
  blocking collectives: 70.8 us -> 0 us
  local copies, waits for them, and re-layouts: 10.1 us -> 80.5 us
  starting transfers between devices: 0.42 us -> 64.9 us
    psum x1 -> x0, waiting for transfers between devices: 952 us -> none  [local(): lax.psum((shares[0], shares[1], shares[2], shares[3], shares[4]), 'dp')]
    reduce_scatter x3 -> x0, waiting for transfers between devices: 753 us -> none  [the longest x1 452 us: local(): lax.psum_scatter(grad_down, 'shard', scatter_dimension=0, tiled=True)]
    all_gather x4 -> x0, waiting for transfers between devices: 628 us -> none  [the longest x1 236 us: local(): lax.all_gather(lowered[2], 'shard', axis=0, tiled=True)]
    pallas_call x0 -> x30, Pallas kernels: none -> 494 us  [the longest x6 156 us: adamw_part(): pl.pallas_call(functools.partial(adamw_kernel, chosen), grid=(steps,), in...]
    unnamed x12 -> x0, waiting for transfers between devices: 452 us -> none
    dot_general x18 -> x0, matrix products: 282 us -> none  [the longest x4 76.3 us: contract_cols(): lax.dot_general(left_side, right_side, (((1,), (1,)), ((), ())), preferre...]
    ppermute x0 -> x70, waiting for transfers between devices: none -> 222 us  [run(): return lax.ppermute(prepare(*values), AXES, pairs)]
    sub x5 -> x1, other arithmetic: 151 us -> 0.66 us  [adamw_step(): master - step_rate * (corrected_m / (jnp.sqrt(corrected_v) + ADAM_EPS) +...]
  transfers between devices with their start and end apart: 10 -> 70, of which waited for: 9 -> 21; matrix products, arithmetic and copies ran while one was open for 9% -> 5% of each run, Pallas kernels for 0% -> 47%
where the time goes in v1:
time: 911 us; the launch traced here: 905 us
  Pallas kernels  494 us (54%)
  waiting for transfers between devices  222 us (24%)
  local copies, waits for them, and re-layouts  80.5 us (9%)
  starting transfers between devices  64.9 us (7%)
  other arithmetic  40.9 us (4%)
    ppermute x70, waiting for transfers between devices, run(): return lax.ppermute(prepare(*values), AXES, pairs)  222 us
    pallas_call x6, Pallas kernels, adamw_part(): pl.pallas_call(functools.partial(adamw_kernel, chosen), grid=(steps,), in...  156 us
    pallas_call x8, Pallas kernels, weighted(): pl.pallas_call(body, in_specs=weights.specs() + specs, scratch_shapes=wei...  149 us
    pallas_call x8, Pallas kernels, outer_products(): pl.pallas_call(functools.partial(outer_kernel, bool(extra)), grid_spec=pl...  97.4 us
    ppermute x70, starting transfers between devices, run(): return lax.ppermute(prepare(*values), AXES, pairs)  64.9 us
    unnamed x136, local copies, waits for them, and re-layouts  48.5 us
    pallas_call x3, Pallas kernels, column_blocks(): pl.pallas_call(functools.partial(blocks_kernel, counts), grid=(rows // st...  41.2 us
    convert_element_type x16, other arithmetic, add_low(): return total.astype(BF16)  32.4 us
  transfers between devices with their start and end apart: 70, of which 21 were waited for; matrix products, arithmetic and copies ran while one was open for 5% of the time, Pallas kernels for 47%

profile of v1, /device:TPU:0, one launch (start us, length us, event | category | flops | bytes accessed | tf_op | source)
XLA Modules:
  0.0 904.7 jit_solution(9305724431344829703)
XLA Ops:
  0.7 5.0 fusion.8
  8.7 14.2 %cast.3.refs_1_ = bf16[4,800,1600]{2,1,0:T(8,128)(2,1)} custom-call(f32[800,6400]{1,0:T(8,128)} %w_ref.6), custom_call_target="tpu_custom_call" | custom-call | flops 1 | bytes 1 | tf_op jit(solution)/shard_map/u_own/cast/pallas_call | solution.py:380
  25.4 12.6 %collective-permute-done.refs_2_ = bf16[400,1600]{1,0:T(8,128)(2,1)S(1)} collective-permute-done((bf16[400,1600]{1,0:T(8,128)(2,1)S(1)}, bf16[400,1600]{1,0:T(8,128)(2,1)S(1)}, u32[]{:S(2)}, u32[]{:S(2)}) %collective-permute-start) | collective-permute-done | bytes 1280032 | tf_op jit(solution)/shard_map/q_g_x/ppermute | solution.py:937
  39.7 14.2 %cast.4.refs_1_ = bf16[2,1600,1600]{2,1,0:T(8,128)(2,1)} custom-call(f32[1600,3200]{1,0:T(8,128)} %bitcast.235), custom_call_target="tpu_custom_call" | custom-call | flops 1 | bytes 1 | tf_op jit(solution)/shard_map/d_own/cast/pallas_call | solution.py:380
  64.7 7.4 collective-permute-done.6.refs_6_
  72.0 14.3 %collective-permute-done.11.refs_8_ = bf16[400,1600]{1,0:T(8,128)(2,1)} collective-permute-done((bf16[400,1600]{1,0:T(8,128)(2,1)}, bf16[400,1600]{1,0:T(8,128)(2,1)}, u32[]{:S(2)}, u32[]{:S(2)}) %collective-permute-start.11) | collective-permute-done | bytes 1280032 | tf_op jit(solution)/shard_map/q_g_ab/ppermute | solution.py:937
  88.8 12.9 %cast.5.refs_1_ = bf16[4,800,1600]{2,1,0:T(8,128)(2,1)} custom-call(f32[800,4800]{1,0:T(8,128)} %w_ref.7, f32[800,1600]{1,0:T(8,128)S(1)} %copy-done.13), custom_call_target="tpu_custom_call" | custom-call | flops 1 | bytes 1 | tf_op jit(solution)/shard_map/q_own/cast/pallas_call | solution.py:380
  110.7 15.9 %project.1.qkv_ref = bf16[3,512,1600]{2,1,0:T(8,128)(2,1)} custom-call(s32[4]{0:T(128)S(1)} %pad_add_fusion.10.refs_0_, bf16[4,800,1600]{2,1,0:T(8,128)(2,1)} %cast.5.refs_1_, bf16[400,1600]{1,0:T(8,128)(2,1)S(1)} %collective-permute-done.refs_2_, bf16[400,1600]{1,0:T(8,128)(2,1)S(1)} %copy-done.16, bf16[400,1600]{1,0:T(8,128)(2,1)} %collective-permute-done.7.refs_4_, ...), custom_call_target="tpu_custom_call" | custom-call | flops 1 | bytes 1 | tf_op jit(solution)/shard_map/project/project/pallas_call | solution.py:407
  126.7 7.8 collective-permute-done.2.refs_2_
  141.3 17.0 %attend.1 = (bf16[512,1600]{1,0:T(8,128)(2,1)S(1)}, f32[512,128]{1,0:T(8,128)S(1)}) custom-call(bf16[3,512,1600]{2,1,0:T(8,128)(2,1)S(1)} %copy-done.4, f32[512,512]{1,0:T(8,128)S(1)} %fusion.18.fill_ref), custom_call_target="tpu_custom_call" | custom-call | flops 1 | bytes 1 | tf_op jit(solution)/shard_map/attend/attend/pallas_call | solution.py:764
  159.6 11.8 %out.1 = (f32[512,1600]{1,0:T(8,128)}, bf16[512,1600]{1,0:T(8,128)(2,1)}) custom-call(s32[4]{0:T(128)S(1)} %pad_add_fusion.10.refs_0_, bf16[4,800,1600]{2,1,0:T(8,128)(2,1)} %cast.5.refs_1_, bf16[400,1600]{1,0:T(8,128)(2,1)S(1)} %collective-permute-done.refs_2_, bf16[400,1600]{1,0:T(8,128)(2,1)S(1)} %copy-done.16, ...), custom_call_target="tpu_custom_call" | custom-call | flops 1 | bytes 1 | tf_op jit(solution)/shard_map/out/out/pallas_call | solution.py:407
  177.2 23.6 %up.1 = (bf16[4,512,1600]{2,1,0:T(8,128)(2,1)}, f32[4,512,1600]{2,1,0:T(8,128)}) custom-call(s32[4]{0:T(128)S(1)} %pad_add_fusion.10.refs_0_, bf16[4,800,1600]{2,1,0:T(8,128)(2,1)} %cast.3.refs_1_, bf16[400,1600]{1,0:T(8,128)(2,1)} %collective-permute-done.3.refs_2_, bf16[400,1600]{1,0:T(8,128)(2,1)S(1)} %copy-done.41, ...), custom_call_target="tpu_custom_call" | custom-call | flops 1 | bytes 1 | tf_op jit(solution)/shard_map/up/up/pallas_call | solution.py:407
  207.5 12.3 %outer.8 = bf16[2,1600,1600]{2,1,0:T(8,128)(2,1)} custom-call(s32[4]{0:T(128)S(1)} %fusion.21.places_ref, bf16[1,512,1600]{2,1,0:T(8,128)(2,1)S(1)} %bitcast.219, bf16[4,512,1600]{2,1,0:T(8,128)(2,1)S(1)} %copy-done.7), custom_call_target="tpu_custom_call" | custom-call | flops 1 | bytes 1 | tf_op jit(solution)/shard_map/d_s/outer/pallas_call | solution.py:710
  221.5 21.6 %layer.1 = bf16[1600,512]{1,0:T(8,128)(2,1)} custom-call(s32[4]{0:T(128)S(1)} %pad_add_fusion.10.refs_0_, bf16[2,1600,1600]{2,1,0:T(8,128)(2,1)} %cast.4.refs_1_, bf16[400,1600]{1,0:T(8,128)(2,1)} %collective-permute-done.2.refs_2_, bf16[400,1600]{1,0:T(8,128)(2,1)S(1)} %copy-done.32, bf16[400,1600]{1,0:T(8,128)(2,1)} %collective-permute-done.18.refs_4_, ...), custom_call_target="tpu_custom_call" | custom-call | flops 1 | bytes 1 | tf_op jit(solution)/shard_map/layer/layer/pallas_call | solution.py:407
  243.2 16.6 %outer.9 = bf16[2,1600,1600]{2,1,0:T(8,128)(2,1)} custom-call(s32[4]{0:T(128)S(1)} %get-tuple-element.928.places_ref, bf16[1,512,1600]{2,1,0:T(8,128)(2,1)S(1)} %bitcast.220, bf16[4,512,1600]{2,1,0:T(8,128)(2,1)S(1)} %bitcast.210, bf16[2,1600,1600]{2,1,0:T(8,128)(2,1)} %collective-permute-done.25.refs_0_), custom_call_target="tpu_custom_call" | custom-call | flops 1 | bytes 1 | tf_op jit(solution)/shard_map/d_k/outer/pallas_call | solution.py:710
  259.9 5.3 dynamic-slice_bitcast_fusion.2
  266.9 21.2 %g_pre.1 = (bf16[4,512,1600]{2,1,0:T(8,128)(2,1)}, f32[4,1,1600]{2,1,0:T(1,128)S(1)}) custom-call(s32[4]{0:T(128)S(1)} %pad_add_fusion.10.refs_0_, bf16[2,1600,1600]{2,1,0:T(8,128)(2,1)} %cast.4.refs_1_, bf16[400,1600]{1,0:T(8,128)(2,1)} %collective-permute-done.2.refs_2_, bf16[400,1600]{1,0:T(8,128)(2,1)S(1)} %copy-done.33, ...), custom_call_target="tpu_custom_call" | custom-call | flops 1 | bytes 1 | tf_op jit(solution)/shard_map/g_pre/g_pre/pallas_call | solution.py:407
  291.1 20.5 %outer.10 = bf16[2,1600,1600]{2,1,0:T(8,128)(2,1)} custom-call(s32[4]{0:T(128)S(1)} %fusion.24.places_ref, bf16[1,512,1600]{2,1,0:T(8,128)(2,1)S(1)} %bitcast.229, bf16[4,512,1600]{2,1,0:T(8,128)(2,1)S(1)} %copy-done.5), custom_call_target="tpu_custom_call" | custom-call | flops 1 | bytes 1 | tf_op jit(solution)/shard_map/u_s/outer/pallas_call | solution.py:710
  318.6 25.5 %n2_b.1 = (f32[512,1600]{1,0:T(8,128)}, bf16[512,1600]{1,0:T(8,128)(2,1)}, f32[8,1600]{1,0:T(8,128)S(1)}) custom-call(s32[4]{0:T(128)S(1)} %pad_add_fusion.10.refs_0_, bf16[4,800,1600]{2,1,0:T(8,128)(2,1)} %cast.3.refs_1_, bf16[400,1600]{1,0:T(8,128)(2,1)} %collective-permute-done.3.refs_2_, bf16[400,1600]{1,0:T(8,128)(2,1)S(1)} %copy-done.42, ...), custom_call_target="tpu_custom_call" | custom-call | flops 1 | bytes 1 | tf_op jit(solution)/shard_map/n2_b/n2_b/pallas_call | solution.py:407
  352.9 16.6 %outer.11 = bf16[2,1600,1600]{2,1,0:T(8,128)(2,1)} custom-call(s32[4]{0:T(128)S(1)} %get-tuple-element.927.places_ref, bf16[1,512,1600]{2,1,0:T(8,128)(2,1)S(1)} %bitcast.230, bf16[4,512,1600]{2,1,0:T(8,128)(2,1)S(1)} %copy-done.6, bf16[2,1600,1600]{2,1,0:T(8,128)(2,1)} %collective-permute-done.28.refs_0_), custom_call_target="tpu_custom_call" | custom-call | flops 1 | bytes 1 | tf_op jit(solution)/shard_map/u_k/outer/pallas_call | solution.py:710
  369.6 5.4 dynamic-slice_bitcast_fusion
  375.6 8.8 g_att.1.grad_ref
  385.8 14.3 %attend_b.2.refs_0_ = bf16[3,512,1600]{2,1,0:T(8,128)(2,1)S(1)} custom-call(bf16[3,512,1600]{2,1,0:T(8,128)(2,1)} %project.1.qkv_ref, bf16[512,1600]{1,0:T(8,128)(2,1)S(1)} %copy-done.25, f32[512,512]{1,0:T(8,128)S(1)} %copy-done.20, f32[512,128]{1,0:T(8,128)S(1)} %get-tuple-element.663.lse_ref), custom_call_target="tpu_custom_call" | custom-call | flops 1 | bytes 1 | tf_op jit(solution)/shard_map/att_b/attend_b/pallas_call | solution.py:829
  400.2 6.1 fusion.4
  413.5 16.4 %attend_b.3.right_ref.refs_10_ = bf16[3,512,1600]{2,1,0:T(8,128)(2,1)S(1)} custom-call(bf16[3,512,1600]{2,1,0:T(8,128)(2,1)} %project.1.qkv_ref, bf16[512,1600]{1,0:T(8,128)(2,1)S(1)} %copy-done.26, f32[512,512]{1,0:T(8,128)S(1)} %copy-done.21, f32[512,128]{1,0:T(8,128)S(1)} %get-tuple-element.663.lse_ref, ...), custom_call_target="tpu_custom_call", output_to_operand_aliasing={{}: (4, {})} | custom-call | flops 1 | bytes 1 | tf_op jit(solution)/shard_map/att_b/attend_b/pallas_call | solution.py:829
  433.7 4.8 fusion.2
  440.7 6.8 outer.12
  447.5 6.8 outer.13
  460.8 20.6 %n1_b.1 = (bf16[1600,512]{1,0:T(8,128)(2,1)}, f32[8,1600]{1,0:T(8,128)S(1)}) custom-call(s32[4]{0:T(128)S(1)} %pad_add_fusion.10.refs_0_, bf16[4,800,1600]{2,1,0:T(8,128)(2,1)} %cast.5.refs_1_, bf16[400,1600]{1,0:T(8,128)(2,1)S(1)} %collective-permute-done.refs_2_, bf16[400,1600]{1,0:T(8,128)(2,1)S(1)} %copy-done.18, ...), custom_call_target="tpu_custom_call" | custom-call | flops 1 | bytes 1 | tf_op jit(solution)/shard_map/n1_b/n1_b/pallas_call | solution.py:407
  483.1 8.4 outer.14
  491.5 24.2 %collective-permute-done.33 = bf16[2,400,1600]{2,1,0:T(8,128)(2,1)} collective-permute-done((bf16[2,400,1600]{2,1,0:T(8,128)(2,1)}, bf16[2,400,1600]{2,1,0:T(8,128)(2,1)}, u32[]{:S(2)}, u32[]{:S(2)}) %collective-permute-start.33) | collective-permute-done | bytes 2560032 | tf_op jit(solution)/shard_map/usc/ppermute | solution.py:937
  532.3 9.4 %outer.15 = bf16[1,1600,1600]{2,1,0:T(8,128)(2,1)} custom-call(s32[2]{0:T(128)S(1)} %pad_add_fusion.8.places_ref, bf16[1,512,1600]{2,1,0:T(8,128)(2,1)S(1)} %bitcast.218, bf16[3,512,1600]{2,1,0:T(8,128)(2,1)S(1)} %copy-done.3, bf16[1,1600,1600]{2,1,0:T(8,128)(2,1)} %collective-permute-done.35.refs_0_), custom_call_target="tpu_custom_call" | custom-call | flops 1 | bytes 1 | tf_op jit(solution)/shard_map/b_k/outer/pallas_call | solution.py:710
  549.6 9.4 %collective-permute-done.38 = bf16[2,200,1600]{2,1,0:T(8,128)(2,1)} collective-permute-done((bf16[2,200,1600]{2,1,0:T(8,128)(2,1)}, bf16[2,200,1600]{2,1,0:T(8,128)(2,1)}, u32[]{:S(2)}, u32[]{:S(2)}) %collective-permute-start.38) | collective-permute-done | bytes 1280032 | tf_op jit(solution)/shard_map/usd/ppermute | solution.py:937
  567.6 19.1 %collective-permute-done.46 = bf16[2,200,1600]{2,1,0:T(8,128)(2,1)S(1)} collective-permute-done((bf16[2,200,1600]{2,1,0:T(8,128)(2,1)S(1)}, bf16[2,200,1600]{2,1,0:T(8,128)(2,1)S(1)}, u32[]{:S(2)}, u32[]{:S(2)}) %collective-permute-start.46) | collective-permute-done | bytes 1280032 | tf_op jit(solution)/shard_map/dgp/ppermute | solution.py:937
  588.8 12.1 %collective-permute-done.43 = bf16[1,400,1600]{2,1,0:T(8,128)(2,1)S(1)} collective-permute-done((bf16[1,400,1600]{2,1,0:T(8,128)(2,1)S(1)}, bf16[1,400,1600]{2,1,0:T(8,128)(2,1)S(1)}, u32[]{:S(2)}, u32[]{:S(2)}) %collective-permute-start.43) | collective-permute-done | bytes 1280032 | tf_op jit(solution)/shard_map/asc/ppermute | solution.py:937
  602.0 13.8 %collective-permute-done.44 = f32[6,1600]{1,0:T(8,128)S(1)} collective-permute-done((f32[6,1600]{1,0:T(8,128)S(1)}, f32[6,1600]{1,0:T(8,128)S(1)}, u32[]{:S(2)}, u32[]{:S(2)}) %collective-permute-start.44) | collective-permute-done | bytes 38432 | tf_op jit(solution)/shard_map/v_dp/ppermute | solution.py:937
  617.4 30.0 %collective-permute-done.49 = bf16[1,400,1600]{2,1,0:T(8,128)(2,1)S(1)} collective-permute-done((bf16[1,400,1600]{2,1,0:T(8,128)(2,1)S(1)}, bf16[1,400,1600]{2,1,0:T(8,128)(2,1)S(1)}, u32[]{:S(2)}, u32[]{:S(2)}) %collective-permute-start.49) | collective-permute-done | bytes 1280032 | tf_op jit(solution)/shard_map/bsc/ppermute | solution.py:937
  648.5 10.2 %collective-permute-start.56 = (bf16[2,800,1600]{2,1,0:T(8,128)(2,1)S(1)}, bf16[2,800,1600]{2,1,0:T(8,128)(2,1)S(1)}, u32[]{:S(2)}, u32[]{:S(2)}) collective-permute-start(bf16[2,800,1600]{2,1,0:T(8,128)(2,1)S(1)} %bitcast.211), channel_id=1, source_target_pairs={{0,2},{1,3},{2,0},{3,1},{4,6},{5,7},{6,4},{7,5},{8,10},{9,11},{10,... | collective-permute-start | bytes 15360008 | tf_op jit(solution)/shard_map/dgc/ppermute | solution.py:937
  662.2 15.4 %collective-permute-done.53 = bf16[1,200,1600]{2,1,0:T(8,128)(2,1)S(1)} collective-permute-done((bf16[1,200,1600]{2,1,0:T(8,128)(2,1)S(1)}, bf16[1,200,1600]{2,1,0:T(8,128)(2,1)S(1)}, u32[]{:S(2)}, u32[]{:S(2)}) %collective-permute-start.53) | collective-permute-done | bytes 640032 | tf_op jit(solution)/shard_map/asd/ppermute | solution.py:937
  681.4 15.8 %collective-permute-done.57 = f32[6,1600]{1,0:T(8,128)S(1)} collective-permute-done((f32[6,1600]{1,0:T(8,128)S(1)}, f32[6,1600]{1,0:T(8,128)S(1)}, u32[]{:S(2)}, u32[]{:S(2)}) %collective-permute-start.57) | collective-permute-done | bytes 38432 | tf_op jit(solution)/shard_map/v_dp/ppermute | solution.py:937
  699.7 25.4 %adamw.6 = (f32[1600,3200]{1,0:T(8,128)}, f32[1600,3200]{1,0:T(8,128)}, f32[1600,3200]{1,0:T(8,128)}) custom-call(s32[1]{0:T(128)} %bitcast.1.core_ref, f32[1600,3200]{1,0:T(8,128)} %bitcast.236, f32[1600,3200]{1,0:T(8,128)} %bitcast.240, f32[1600,3200]{1,0:T(8,128)} %bitcast.242, bf16[2,800,1600]{2,1,0:T(8,128)(2,1)S(1)} %bitcast.212, ...), custom_call_target="tpu_custom_call" | custom-call | flops 1 | bytes 1 | tf_op jit(solution)/shard_map/n_d/adamw/pallas_call | solution.py:889
  731.1 25.4 %adamw.7 = (f32[1600,3200]{1,0:T(8,128)}, f32[1600,3200]{1,0:T(8,128)}, f32[1600,3200]{1,0:T(8,128)}) custom-call(s32[1]{0:T(128)} %bitcast.1.core_ref, f32[1600,3200]{1,0:T(8,128)} %bitcast.237, f32[1600,3200]{1,0:T(8,128)} %bitcast.241, f32[1600,3200]{1,0:T(8,128)} %bitcast.243, ...), custom_call_target="tpu_custom_call", output_to_operand_aliasing={{0}: (6, {}), {1}: (7, {}), {2}: (8, {})} | custom-call | flops 1 | bytes 1 | tf_op jit(solution)/shard_map/n_d/adamw/pallas_call | solution.py:889
  756.5 17.6 %collective-permute-done.61 = bf16[1,200,1600]{2,1,0:T(8,128)(2,1)S(1)} collective-permute-done((bf16[1,200,1600]{2,1,0:T(8,128)(2,1)S(1)}, bf16[1,200,1600]{2,1,0:T(8,128)(2,1)S(1)}, u32[]{:S(2)}, u32[]{:S(2)}) %collective-permute-start.61) | collective-permute-done | bytes 640032 | tf_op jit(solution)/shard_map/agq/ppermute | solution.py:937
  776.0 8.9 collective-permute-done.63
  788.4 25.4 %adamw.8 = (f32[800,6400]{1,0:T(8,128)}, f32[800,6400]{1,0:T(8,128)}, f32[800,6400]{1,0:T(8,128)}) custom-call(s32[1]{0:T(128)} %bitcast.1.core_ref, f32[800,6400]{1,0:T(8,128)} %w_ref.6, f32[800,6400]{1,0:T(8,128)} %m_ref.6, f32[800,6400]{1,0:T(8,128)} %v_ref.6, bf16[2,800,1600]{2,1,0:T(8,128)(2,1)S(1)} %bitcast.215, bf16[2,800,1600]{2,1,0:T(8,128)(2,1)} %copy-done.46), custom_call_target="tpu_custom_call" | custom-call | flops 1 | bytes 1 | tf_op jit(solution)/shard_map/n_u/adamw/pallas_call | solution.py:889
  815.9 15.7 %adamw.9 = (f32[800,1600]{1,0:T(8,128)}, f32[800,1600]{1,0:T(8,128)}, f32[800,1600]{1,0:T(8,128)}) custom-call(s32[1]{0:T(128)} %bitcast.1.core_ref, f32[800,1600]{1,0:T(8,128)} %w_ref.5, f32[800,1600]{1,0:T(8,128)} %m_ref.5, f32[800,1600]{1,0:T(8,128)} %v_ref.5, bf16[1,800,1600]{2,1,0:T(8,128)(2,1)S(1)} %bitcast.222, ...), custom_call_target="tpu_custom_call" | custom-call | flops 1 | bytes 1 | tf_op jit(solution)/shard_map/n_o/adamw/pallas_call | solution.py:889
  840.3 25.6 %adamw.10 = (f32[800,6400]{1,0:T(8,128)}, f32[800,6400]{1,0:T(8,128)}, f32[800,6400]{1,0:T(8,128)}) custom-call(s32[1]{0:T(128)} %bitcast.1.core_ref, f32[800,6400]{1,0:T(8,128)} %w_ref.6, f32[800,6400]{1,0:T(8,128)} %m_ref.6, f32[800,6400]{1,0:T(8,128)} %v_ref.6, ...), custom_call_target="tpu_custom_call", output_to_operand_aliasing={{0}: (6, {}), {1}: (7, {}), {2}: (8, {})} | custom-call | flops 1 | bytes 1 | tf_op jit(solution)/shard_map/n_u/adamw/pallas_call | solution.py:889
  865.9 38.7 %adamw.11 = (f32[800,4800]{1,0:T(8,128)}, f32[800,4800]{1,0:T(8,128)}, f32[800,4800]{1,0:T(8,128)}) custom-call(s32[1]{0:T(128)} %bitcast.1.core_ref, f32[800,4800]{1,0:T(8,128)} %w_ref.7, f32[800,4800]{1,0:T(8,128)} %m_ref.7, f32[800,4800]{1,0:T(8,128)} %v_ref.7, bf16[1,800,1600]{2,1,0:T(8,128)(2,1)S(1)} %bitcast.223, bf16[1,800,1600]{2,1,0:T(8,128)(2,1)S(1)} %copy-done.29, ...), custom_call_target="tpu_custom_call" | custom-call | flops 1 | bytes 1 | tf_op jit(solution)/shard_map/n_q/adamw/pallas_call | solution.py:889
  (361 shorter events, 165.7 us)
Async XLA Ops:
  5.7 32.2 %collective-permute-start = (bf16[400,1600]{1,0:T(8,128)(2,1)S(1)}, bf16[400,1600]{1,0:T(8,128)(2,1)S(1)}, u32[]{:S(2)}, u32[]{:S(2)}) collective-permute-start(bf16[400,1600]{1,0:T(8,128)(2,1)S(1)} %fusion.8), channel_id=1, source_target_pairs={{0,1},{1,0},{2,3},{3,2},{4,5},{5,4},{6,7},{7,6},{8,9},{9,8},{10,11... | collective-permute-start | bytes 3840008 | tf_op jit(solution)/shard_map/q_g_x/ppermute | solution.py:937
  62.7 23.6 %collective-permute-start.11 = (bf16[400,1600]{1,0:T(8,128)(2,1)}, bf16[400,1600]{1,0:T(8,128)(2,1)}, u32[]{:S(2)}, u32[]{:S(2)}) collective-permute-start(bf16[400,1600]{1,0:T(8,128)(2,1)} %collective-permute-done.7.refs_4_), channel_id=1, source_target_pairs={{0,8},{1,9},{2,6},{3,7},{4,12},{5,13},{6,2},{7,3},{8,0},{9,1},{10,... | collective-permute-start | bytes 3840008 | tf_op jit(solution)/shard_map/q_g_ab/ppermute | solution.py:937
  63.1 40.9 %collective-permute-start.3 = (bf16[400,1600]{1,0:T(8,128)(2,1)}, bf16[400,1600]{1,0:T(8,128)(2,1)}, u32[]{:S(2)}, u32[]{:S(2)}) collective-permute-start(bf16[400,1600]{1,0:T(8,128)(2,1)} %dynamic-slice_bitcast_fusion.13), channel_id=1, source_target_pairs={{0,1},{1,0},{2,3},{3,2},{4,5},{5,4},{6,7},{7,6},{8,9},{9,8},{10,11... | collective-permute-start | bytes 3840008 | tf_op jit(solution)/shard_map/u_g_x/ppermute | solution.py:937
  64.6 40.6 %collective-permute-start.9 = (bf16[400,1600]{1,0:T(8,128)(2,1)}, bf16[400,1600]{1,0:T(8,128)(2,1)}, u32[]{:S(2)}, u32[]{:S(2)}) collective-permute-start(bf16[400,1600]{1,0:T(8,128)(2,1)} %collective-permute-done.7.refs_4_), channel_id=1, source_target_pairs={{0,2},{1,3},{2,0},{3,1},{4,6},{5,7},{6,4},{7,5},{8,10},{9,11},{10,... | collective-permute-start | bytes 3840008 | tf_op jit(solution)/shard_map/q_g_ac/ppermute | solution.py:937
  72.0 38.6 %collective-permute-start.10 = (bf16[400,1600]{1,0:T(8,128)(2,1)}, bf16[400,1600]{1,0:T(8,128)(2,1)}, u32[]{:S(2)}, u32[]{:S(2)}) collective-permute-start(bf16[400,1600]{1,0:T(8,128)(2,1)} %collective-permute-done.6.refs_6_), channel_id=1, source_target_pairs={{0,2},{1,3},{2,0},{3,1},{4,6},{5,7},{6,4},{7,5},{8,10},{9,11},{10,... | collective-permute-start | bytes 3840008 | tf_op jit(solution)/shard_map/q_g_bc/ppermute | solution.py:937
  86.3 24.3 %collective-permute-start.12 = (bf16[400,1600]{1,0:T(8,128)(2,1)}, bf16[400,1600]{1,0:T(8,128)(2,1)}, u32[]{:S(2)}, u32[]{:S(2)}) collective-permute-start(bf16[400,1600]{1,0:T(8,128)(2,1)} %collective-permute-done.11.refs_8_), channel_id=1, source_target_pairs={{0,2},{1,3},{2,0},{3,1},{4,6},{5,7},{6,4},{7,5},{8,10},{9,11},{10,... | collective-permute-start | bytes 3840008 | tf_op jit(solution)/shard_map/q_g_abc/ppermute | solution.py:937
  102.5 32.0 %collective-permute-start.2 = (bf16[400,1600]{1,0:T(8,128)(2,1)}, bf16[400,1600]{1,0:T(8,128)(2,1)}, u32[]{:S(2)}, u32[]{:S(2)}) collective-permute-start(bf16[400,1600]{1,0:T(8,128)(2,1)} %dynamic-slice_bitcast_fusion.12), channel_id=1, source_target_pairs={{0,1},{1,0},{2,3},{3,2},{4,5},{5,4},{6,7},{7,6},{8,9},{9,8},{10,11... | collective-permute-start | bytes 3840008 | tf_op jit(solution)/shard_map/d_g_x/ppermute | solution.py:937
  104.1 31.6 %collective-permute-start.4 = (bf16[400,1600]{1,0:T(8,128)(2,1)}, bf16[400,1600]{1,0:T(8,128)(2,1)}, u32[]{:S(2)}, u32[]{:S(2)}) collective-permute-start(bf16[400,1600]{1,0:T(8,128)(2,1)} %collective-permute-done.3.refs_2_), channel_id=1, source_target_pairs={{0,4},{1,5},{2,10},{3,11},{4,0},{5,1},{6,14},{7,15},{8,12},{9,13},... | collective-permute-start | bytes 3840008 | tf_op jit(solution)/shard_map/u_g_a/ppermute | solution.py:937
  105.3 30.4 %collective-permute-start.5 = (bf16[400,1600]{1,0:T(8,128)(2,1)}, bf16[400,1600]{1,0:T(8,128)(2,1)S(1)}, u32[]{:S(2)}, u32[]{:S(2)}) collective-permute-start(bf16[400,1600]{1,0:T(8,128)(2,1)} %collective-permute-done.3.refs_2_), channel_id=1, source_target_pairs={{0,8},{1,9},{2,6},{3,7},{4,12},{5,13},{6,2},{7,3},{8,0},{9,1},{10,... | collective-permute-start | bytes 3840008 | tf_op jit(solution)/shard_map/u_g_b/ppermute | solution.py:937
  135.6 23.9 %collective-permute-start.13 = (bf16[400,1600]{1,0:T(8,128)(2,1)}, bf16[400,1600]{1,0:T(8,128)(2,1)S(1)}, u32[]{:S(2)}, u32[]{:S(2)}) collective-permute-start(bf16[400,1600]{1,0:T(8,128)(2,1)} %collective-permute-done.2.refs_2_), channel_id=1, source_target_pairs={{0,2},{1,3},{2,0},{3,1},{4,6},{5,7},{6,4},{7,5},{8,10},{9,11},{10,... | collective-permute-start | bytes 3840008 | tf_op jit(solution)/shard_map/d_g_xc/ppermute | solution.py:937
  136.7 34.8 %collective-permute-start.17 = (bf16[400,1600]{1,0:T(8,128)(2,1)}, bf16[400,1600]{1,0:T(8,128)(2,1)}, u32[]{:S(2)}, u32[]{:S(2)}) collective-permute-start(bf16[400,1600]{1,0:T(8,128)(2,1)} %collective-permute-done.4.refs_4_), channel_id=1, source_target_pairs={{0,8},{1,9},{2,6},{3,7},{4,12},{5,13},{6,2},{7,3},{8,0},{9,1},{10,... | collective-permute-start | bytes 3840008 | tf_op jit(solution)/shard_map/u_g_ab/ppermute | solution.py:937
  138.4 33.1 %collective-permute-start.18 = (bf16[400,1600]{1,0:T(8,128)(2,1)}, bf16[400,1600]{1,0:T(8,128)(2,1)}, u32[]{:S(2)}, u32[]{:S(2)}) collective-permute-start(bf16[400,1600]{1,0:T(8,128)(2,1)} %collective-permute-done.2.refs_2_), channel_id=1, source_target_pairs={{0,4},{1,5},{2,10},{3,11},{4,0},{5,1},{6,14},{7,15},{8,12},{9,13},... | collective-permute-start | bytes 3840008 | tf_op jit(solution)/shard_map/d_g_a/ppermute | solution.py:937
  171.5 29.4 %collective-permute-start.19 = (bf16[400,1600]{1,0:T(8,128)(2,1)}, bf16[400,1600]{1,0:T(8,128)(2,1)}, u32[]{:S(2)}, u32[]{:S(2)}) collective-permute-start(bf16[400,1600]{1,0:T(8,128)(2,1)} %collective-permute-done.18.refs_4_), channel_id=1, source_target_pairs={{0,8},{1,9},{2,6},{3,7},{4,12},{5,13},{6,2},{7,3},{8,0},{9,1},{10,... | collective-permute-start | bytes 3840008 | tf_op jit(solution)/shard_map/d_g_ab/ppermute | solution.py:937
  172.4 31.6 %collective-permute-start.16 = (bf16[400,1600]{1,0:T(8,128)(2,1)}, bf16[400,1600]{1,0:T(8,128)(2,1)}, u32[]{:S(2)}, u32[]{:S(2)}) collective-permute-start(bf16[400,1600]{1,0:T(8,128)(2,1)} %collective-permute-done.2.refs_2_), channel_id=1, source_target_pairs={{0,8},{1,9},{2,6},{3,7},{4,12},{5,13},{6,2},{7,3},{8,0},{9,1},{10,... | collective-permute-start | bytes 3840008 | tf_op jit(solution)/shard_map/d_g_b/ppermute | solution.py:937
  174.7 45.1 %collective-permute-start.22 = (bf16[400,1600]{1,0:T(8,128)(2,1)}, bf16[400,1600]{1,0:T(8,128)(2,1)}, u32[]{:S(2)}, u32[]{:S(2)}) collective-permute-start(bf16[400,1600]{1,0:T(8,128)(2,1)} %collective-permute-done.18.refs_4_), channel_id=1, source_target_pairs={{0,2},{1,3},{2,0},{3,1},{4,6},{5,7},{6,4},{7,5},{8,10},{9,11},{10,... | collective-permute-start | bytes 3840008 | tf_op jit(solution)/shard_map/d_g_ac/ppermute | solution.py:937
  265.2 46.3 %collective-permute-start.26 = (bf16[2,400,1600]{2,1,0:T(8,128)(2,1)}, bf16[2,400,1600]{2,1,0:T(8,128)(2,1)}, u32[]{:S(2)}, u32[]{:S(2)}) collective-permute-start(bf16[2,400,1600]{2,1,0:T(8,128)(2,1)} %get-tuple-element.610), channel_id=1, source_target_pairs={{0,1},{1,0},{2,10},{3,11},{4,5},{5,4},{6,14},{7,15},{8,9},{9,8},{1... | collective-permute-start | bytes 7680008 | tf_op jit(solution)/shard_map/dsa/ppermute | solution.py:937
  311.5 37.4 %collective-permute-start.28 = (bf16[2,1600,1600]{2,1,0:T(8,128)(2,1)}, bf16[2,1600,1600]{2,1,0:T(8,128)(2,1)}, u32[]{:S(2)}, u32[]{:S(2)}) collective-permute-start(bf16[2,1600,1600]{2,1,0:T(8,128)(2,1)} %outer.10), channel_id=1, source_target_pairs={{0,2},{1,3},{2,0},{3,1},{4,6},{5,7},{6,4},{7,5},{8,10},{9,11},{10,... | collective-permute-start | bytes 30720008 | tf_op jit(solution)/shard_map/u_c/ppermute | solution.py:937
  312.3 36.6 %collective-permute-start.27 = (bf16[2,400,1600]{2,1,0:T(8,128)(2,1)}, bf16[2,400,1600]{2,1,0:T(8,128)(2,1)}, u32[]{:S(2)}, u32[]{:S(2)}) collective-permute-start(bf16[2,400,1600]{2,1,0:T(8,128)(2,1)} %get-tuple-element.614), channel_id=1, source_target_pairs={{0,1},{1,0},{2,10},{3,11},{4,5},{5,4},{6,14},{7,15},{8,9},{9,8},{1... | collective-permute-start | bytes 7680008 | tf_op jit(solution)/shard_map/dsb/ppermute | solution.py:937
  348.9 51.3 %collective-permute-start.30 = (bf16[2,400,1600]{2,1,0:T(8,128)(2,1)}, bf16[2,400,1600]{2,1,0:T(8,128)(2,1)}, u32[]{:S(2)}, u32[]{:S(2)}) collective-permute-start(bf16[2,400,1600]{2,1,0:T(8,128)(2,1)} %fusion.5), channel_id=1, source_target_pairs={{0,4},{1,5},{2,3},{3,2},{4,0},{5,1},{6,7},{7,6},{8,12},{9,13},{10,... | collective-permute-start | bytes 7680008 | tf_op jit(solution)/shard_map/dsc/ppermute | solution.py:937
  375.0 54.9 %collective-permute-start.29 = (bf16[2,400,1600]{2,1,0:T(8,128)(2,1)}, bf16[2,400,1600]{2,1,0:T(8,128)(2,1)}, u32[]{:S(2)}, u32[]{:S(2)}) collective-permute-start(bf16[2,400,1600]{2,1,0:T(8,128)(2,1)} %get-tuple-element.638), channel_id=1, source_target_pairs={{0,1},{1,0},{2,6},{3,7},{4,5},{5,4},{6,2},{7,3},{8,9},{9,8},{10,14... | collective-permute-start | bytes 7680008 | tf_op jit(solution)/shard_map/usa/ppermute | solution.py:937
  454.2 27.2 %collective-permute-start.35 = (bf16[1,1600,1600]{2,1,0:T(8,128)(2,1)}, bf16[1,1600,1600]{2,1,0:T(8,128)(2,1)}, u32[]{:S(2)}, u32[]{:S(2)}) collective-permute-start(bf16[1,1600,1600]{2,1,0:T(8,128)(2,1)} %outer.13), channel_id=1, source_target_pairs={{0,2},{1,3},{2,0},{3,1},{4,6},{5,7},{6,4},{7,5},{8,10},{9,11},{10,... | collective-permute-start | bytes 15360008 | tf_op jit(solution)/shard_map/b_c/ppermute | solution.py:937
  454.2 27.2 %collective-permute-start.34 = (bf16[1,1600,1600]{2,1,0:T(8,128)(2,1)}, bf16[1,1600,1600]{2,1,0:T(8,128)(2,1)}, u32[]{:S(2)}, u32[]{:S(2)}) collective-permute-start(bf16[1,1600,1600]{2,1,0:T(8,128)(2,1)} %outer.12), channel_id=1, source_target_pairs={{0,2},{1,3},{2,0},{3,1},{4,6},{5,7},{6,4},{7,5},{8,10},{9,11},{10,... | collective-permute-start | bytes 15360008 | tf_op jit(solution)/shard_map/a_c/ppermute | solution.py:937
  454.7 60.9 %collective-permute-start.33 = (bf16[2,400,1600]{2,1,0:T(8,128)(2,1)}, bf16[2,400,1600]{2,1,0:T(8,128)(2,1)}, u32[]{:S(2)}, u32[]{:S(2)}) collective-permute-start(bf16[2,400,1600]{2,1,0:T(8,128)(2,1)} %fusion.2), channel_id=1, source_target_pairs={{0,8},{1,9},{2,3},{3,2},{4,12},{5,13},{6,7},{7,6},{8,0},{9,1},{10,... | collective-permute-start | bytes 7680008 | tf_op jit(solution)/shard_map/usc/ppermute | solution.py:937
  455.3 60.4 %collective-permute-start.32 = (bf16[2,400,1600]{2,1,0:T(8,128)(2,1)}, bf16[2,400,1600]{2,1,0:T(8,128)(2,1)}, u32[]{:S(2)}, u32[]{:S(2)}) collective-permute-start(bf16[2,400,1600]{2,1,0:T(8,128)(2,1)} %get-tuple-element.692), channel_id=1, source_target_pairs={{0,1},{1,0},{2,6},{3,7},{4,5},{5,4},{6,2},{7,3},{8,9},{9,8},{10,14... | collective-permute-start | bytes 7680008 | tf_op jit(solution)/shard_map/usb/ppermute | solution.py:937
  456.8 66.1 %collective-permute-start.36 = (bf16[2,200,1600]{2,1,0:T(8,128)(2,1)}, bf16[2,200,1600]{2,1,0:T(8,128)(2,1)}, u32[]{:S(2)}, u32[]{:S(2)}) collective-permute-start(bf16[2,200,1600]{2,1,0:T(8,128)(2,1)} %add_convert_fusion.3), channel_id=1, source_target_pairs={{0,16},{1,17},{2,18},{3,19},{4,20},{5,21},{6,22},{7,23},{8,24},{9,... | collective-permute-start | bytes 3840008 | tf_op jit(solution)/shard_map/dse/ppermute | solution.py:937
  526.5 32.4 %collective-permute-start.38 = (bf16[2,200,1600]{2,1,0:T(8,128)(2,1)}, bf16[2,200,1600]{2,1,0:T(8,128)(2,1)}, u32[]{:S(2)}, u32[]{:S(2)}) collective-permute-start(bf16[2,200,1600]{2,1,0:T(8,128)(2,1)} %get-tuple-element.729), channel_id=1, source_target_pairs={{0,4},{1,5},{2,10},{3,11},{4,0},{5,1},{6,14},{7,15},{8,12},{9,13},... | collective-permute-start | bytes 3840008 | tf_op jit(solution)/shard_map/usd/ppermute | solution.py:937
  527.3 33.5 %collective-permute-start.40 = (bf16[1,400,1600]{2,1,0:T(8,128)(2,1)}, bf16[1,400,1600]{2,1,0:T(8,128)(2,1)}, u32[]{:S(2)}, u32[]{:S(2)}) collective-permute-start(bf16[1,400,1600]{2,1,0:T(8,128)(2,1)} %get-tuple-element.737), channel_id=1, source_target_pairs={{0,1},{1,0},{2,10},{3,11},{4,5},{5,4},{6,14},{7,15},{8,9},{9,8},{1... | collective-permute-start | bytes 3840008 | tf_op jit(solution)/shard_map/asa/ppermute | solution.py:937
  529.8 33.0 %collective-permute-start.42 = (bf16[2,200,1600]{2,1,0:T(8,128)(2,1)}, bf16[2,200,1600]{2,1,0:T(8,128)(2,1)S(1)}, u32[]{:S(2)}, u32[]{:S(2)}) collective-permute-start(bf16[2,200,1600]{2,1,0:T(8,128)(2,1)} %add_convert_fusion.2), channel_id=1, source_target_pairs={{0,8},{1,9},{2,6},{3,7},{4,12},{5,13},{6,2},{7,3},{8,0},{9,1},{10,... | collective-permute-start | bytes 3840008 | tf_op jit(solution)/shard_map/dgq/ppermute | solution.py:937
  548.5 38.2 %collective-permute-start.46 = (bf16[2,200,1600]{2,1,0:T(8,128)(2,1)S(1)}, bf16[2,200,1600]{2,1,0:T(8,128)(2,1)S(1)}, u32[]{:S(2)}, u32[]{:S(2)}) collective-permute-start(bf16[2,200,1600]{2,1,0:T(8,128)(2,1)S(1)} %copy-done.52), channel_id=1, source_target_pairs={{0,4},{1,5},{2,10},{3,11},{4,0},{5,1},{6,14},{7,15},{8,12},{9,13},... | collective-permute-start | bytes 3840008 | tf_op jit(solution)/shard_map/dgp/ppermute | solution.py:937
  562.7 26.1 %collective-permute-start.41 = (bf16[1,400,1600]{2,1,0:T(8,128)(2,1)S(1)}, bf16[1,400,1600]{2,1,0:T(8,128)(2,1)S(1)}, u32[]{:S(2)}, u32[]{:S(2)}) collective-permute-start(bf16[1,400,1600]{2,1,0:T(8,128)(2,1)S(1)} %copy-done.54), channel_id=1, source_target_pairs={{0,1},{1,0},{2,10},{3,11},{4,5},{5,4},{6,14},{7,15},{8,9},{9,8},{1... | collective-permute-start | bytes 3840008 | tf_op jit(solution)/shard_map/asb/ppermute | solution.py:937
  562.8 38.1 %collective-permute-start.43 = (bf16[1,400,1600]{2,1,0:T(8,128)(2,1)S(1)}, bf16[1,400,1600]{2,1,0:T(8,128)(2,1)S(1)}, u32[]{:S(2)}, u32[]{:S(2)}) collective-permute-start(bf16[1,400,1600]{2,1,0:T(8,128)(2,1)S(1)} %fusion.14), channel_id=1, source_target_pairs={{0,4},{1,5},{2,3},{3,2},{4,0},{5,1},{6,7},{7,6},{8,12},{9,13},{10,... | collective-permute-start | bytes 3840008 | tf_op jit(solution)/shard_map/asc/ppermute | solution.py:937
  566.0 49.9 %collective-permute-start.47 = (bf16[2,200,1600]{2,1,0:T(8,128)(2,1)S(1)}, bf16[2,200,1600]{2,1,0:T(8,128)(2,1)S(1)}, u32[]{:S(2)}, u32[]{:S(2)}) collective-permute-start(bf16[2,200,1600]{2,1,0:T(8,128)(2,1)S(1)} %collective-permute-done.42), channel_id=1, source_target_pairs={{0,4},{1,5},{2,10},{3,11},{4,0},{5,1},{6,14},{7,15},{8,12},{9,13},... | collective-permute-start | bytes 3840008 | tf_op jit(solution)/shard_map/dgr/ppermute | solution.py:937
  586.7 60.7 %collective-permute-start.49 = (bf16[1,400,1600]{2,1,0:T(8,128)(2,1)S(1)}, bf16[1,400,1600]{2,1,0:T(8,128)(2,1)S(1)}, u32[]{:S(2)}, u32[]{:S(2)}) collective-permute-start(bf16[1,400,1600]{2,1,0:T(8,128)(2,1)S(1)} %fusion.11), channel_id=1, source_target_pairs={{0,8},{1,9},{2,3},{3,2},{4,12},{5,13},{6,7},{7,6},{8,0},{9,1},{10,... | collective-permute-start | bytes 3840008 | tf_op jit(solution)/shard_map/bsc/ppermute | solution.py:937
  586.7 60.7 %collective-permute-start.48 = (bf16[2,200,1600]{2,1,0:T(8,128)(2,1)S(1)}, bf16[2,200,1600]{2,1,0:T(8,128)(2,1)S(1)}, u32[]{:S(2)}, u32[]{:S(2)}) collective-permute-start(bf16[2,200,1600]{2,1,0:T(8,128)(2,1)S(1)} %add_convert_fusion.1), channel_id=1, source_target_pairs={{0,16},{1,17},{2,18},{3,19},{4,20},{5,21},{6,22},{7,23},{8,24},{9,... | collective-permute-start | bytes 3840008 | tf_op jit(solution)/shard_map/use/ppermute | solution.py:937
  615.8 32.7 %collective-permute-start.50 = (f32[6,1600]{1,0:T(8,128)S(1)}, f32[6,1600]{1,0:T(8,128)S(1)}, u32[]{:S(2)}, u32[]{:S(2)}) collective-permute-start(f32[6,1600]{1,0:T(8,128)S(1)} %add.345), channel_id=1, source_target_pairs={{0,8},{1,9},{2,10},{3,11},{4,12},{5,13},{6,14},{7,15},{8,0},{9,1},... | collective-permute-start | bytes 115208 | tf_op jit(solution)/shard_map/v_dp/ppermute | solution.py:937
  648.5 48.7 %collective-permute-start.56 = (bf16[2,800,1600]{2,1,0:T(8,128)(2,1)S(1)}, bf16[2,800,1600]{2,1,0:T(8,128)(2,1)S(1)}, u32[]{:S(2)}, u32[]{:S(2)}) collective-permute-start(bf16[2,800,1600]{2,1,0:T(8,128)(2,1)S(1)} %bitcast.211), channel_id=1, source_target_pairs={{0,2},{1,3},{2,0},{3,1},{4,6},{5,7},{6,4},{7,5},{8,10},{9,11},{10,... | collective-permute-start | bytes 15360008 | tf_op jit(solution)/shard_map/dgc/ppermute | solution.py:937
  660.3 64.7 %collective-permute-start.51 = (bf16[2,200,1600]{2,1,0:T(8,128)(2,1)S(1)}, bf16[2,200,1600]{2,1,0:T(8,128)(2,1)S(1)}, u32[]{:S(2)}, u32[]{:S(2)}) collective-permute-start(bf16[2,200,1600]{2,1,0:T(8,128)(2,1)S(1)} %add_convert_fusion), channel_id=1, source_target_pairs={{0,8},{1,9},{2,6},{3,7},{4,12},{5,13},{6,2},{7,3},{8,0},{9,1},{10,... | collective-permute-start | bytes 3840008 | tf_op jit(solution)/shard_map/ugp/ppermute | solution.py:937
  662.2 62.9 %collective-permute-start.52 = (bf16[2,200,1600]{2,1,0:T(8,128)(2,1)S(1)}, bf16[2,200,1600]{2,1,0:T(8,128)(2,1)S(1)}, u32[]{:S(2)}, u32[]{:S(2)}) collective-permute-start(bf16[2,200,1600]{2,1,0:T(8,128)(2,1)S(1)} %add_convert_fusion), channel_id=1, source_target_pairs={{0,4},{1,5},{2,10},{3,11},{4,0},{5,1},{6,14},{7,15},{8,12},{9,13},... | collective-permute-start | bytes 3840008 | tf_op jit(solution)/shard_map/ugq/ppermute | solution.py:937
  681.0 44.1 %collective-permute-start.55 = (bf16[1,200,1600]{2,1,0:T(8,128)(2,1)S(1)}, bf16[1,200,1600]{2,1,0:T(8,128)(2,1)S(1)}, u32[]{:S(2)}, u32[]{:S(2)}) collective-permute-start(bf16[1,200,1600]{2,1,0:T(8,128)(2,1)S(1)} %add_convert_fusion.7), channel_id=1, source_target_pairs={{0,16},{1,17},{2,18},{3,19},{4,20},{5,21},{6,22},{7,23},{8,24},{9,... | collective-permute-start | bytes 1920008 | tf_op jit(solution)/shard_map/ase/ppermute | solution.py:937
  697.3 27.8 %collective-permute-start.58 = (bf16[1,200,1600]{2,1,0:T(8,128)(2,1)S(1)}, bf16[1,200,1600]{2,1,0:T(8,128)(2,1)S(1)}, u32[]{:S(2)}, u32[]{:S(2)}) collective-permute-start(bf16[1,200,1600]{2,1,0:T(8,128)(2,1)S(1)} %get-tuple-element.794), channel_id=1, source_target_pairs={{0,4},{1,5},{2,10},{3,11},{4,0},{5,1},{6,14},{7,15},{8,12},{9,13},... | collective-permute-start | bytes 1920008 | tf_op jit(solution)/shard_map/bsd/ppermute | solution.py:937
  725.1 49.0 %collective-permute-start.59 = (bf16[2,200,1600]{2,1,0:T(8,128)(2,1)S(1)}, bf16[2,200,1600]{2,1,0:T(8,128)(2,1)S(1)}, u32[]{:S(2)}, u32[]{:S(2)}) collective-permute-start(bf16[2,200,1600]{2,1,0:T(8,128)(2,1)S(1)} %collective-permute-done.52), channel_id=1, source_target_pairs={{0,8},{1,9},{2,6},{3,7},{4,12},{5,13},{6,2},{7,3},{8,0},{9,1},{10,... | collective-permute-start | bytes 3840008 | tf_op jit(solution)/shard_map/ugr/ppermute | solution.py:937
  730.2 43.9 %collective-permute-start.61 = (bf16[1,200,1600]{2,1,0:T(8,128)(2,1)S(1)}, bf16[1,200,1600]{2,1,0:T(8,128)(2,1)S(1)}, u32[]{:S(2)}, u32[]{:S(2)}) collective-permute-start(bf16[1,200,1600]{2,1,0:T(8,128)(2,1)S(1)} %add_convert_fusion.5), channel_id=1, source_target_pairs={{0,8},{1,9},{2,6},{3,7},{4,12},{5,13},{6,2},{7,3},{8,0},{9,1},{10,... | collective-permute-start | bytes 1920008 | tf_op jit(solution)/shard_map/agq/ppermute | solution.py:937
  730.2 43.9 %collective-permute-start.62 = (bf16[1,200,1600]{2,1,0:T(8,128)(2,1)S(1)}, bf16[1,200,1600]{2,1,0:T(8,128)(2,1)S(1)}, u32[]{:S(2)}, u32[]{:S(2)}) collective-permute-start(bf16[1,200,1600]{2,1,0:T(8,128)(2,1)S(1)} %add_convert_fusion.5), channel_id=1, source_target_pairs={{0,4},{1,5},{2,10},{3,11},{4,0},{5,1},{6,14},{7,15},{8,12},{9,13},... | collective-permute-start | bytes 1920008 | tf_op jit(solution)/shard_map/agp/ppermute | solution.py:937
  730.7 43.4 %collective-permute-start.60 = (bf16[1,200,1600]{2,1,0:T(8,128)(2,1)S(1)}, bf16[1,200,1600]{2,1,0:T(8,128)(2,1)S(1)}, u32[]{:S(2)}, u32[]{:S(2)}) collective-permute-start(bf16[1,200,1600]{2,1,0:T(8,128)(2,1)S(1)} %add_convert_fusion.6), channel_id=1, source_target_pairs={{0,16},{1,17},{2,18},{3,19},{4,20},{5,21},{6,22},{7,23},{8,24},{9,... | collective-permute-start | bytes 1920008 | tf_op jit(solution)/shard_map/bse/ppermute | solution.py:937
  785.4 28.4 %collective-permute-start.66 = (bf16[1,800,1600]{2,1,0:T(8,128)(2,1)S(1)}, bf16[1,800,1600]{2,1,0:T(8,128)(2,1)S(1)}, u32[]{:S(2)}, u32[]{:S(2)}) collective-permute-start(bf16[1,800,1600]{2,1,0:T(8,128)(2,1)S(1)} %bitcast.221), channel_id=1, source_target_pairs={{0,2},{1,3},{2,0},{3,1},{4,6},{5,7},{6,4},{7,5},{8,10},{9,11},{10,... | collective-permute-start | bytes 7680008 | tf_op jit(solution)/shard_map/agc/ppermute | solution.py:937
  785.5 28.3 %collective-permute-start.64 = (bf16[1,200,1600]{2,1,0:T(8,128)(2,1)S(1)}, bf16[1,200,1600]{2,1,0:T(8,128)(2,1)S(1)}, u32[]{:S(2)}, u32[]{:S(2)}) collective-permute-start(bf16[1,200,1600]{2,1,0:T(8,128)(2,1)S(1)} %add_convert_fusion.4), channel_id=1, source_target_pairs={{0,4},{1,5},{2,10},{3,11},{4,0},{5,1},{6,14},{7,15},{8,12},{9,13},... | collective-permute-start | bytes 1920008 | tf_op jit(solution)/shard_map/bgq/ppermute | solution.py:937
  786.0 27.8 %collective-permute-start.65 = (bf16[1,200,1600]{2,1,0:T(8,128)(2,1)S(1)}, bf16[1,200,1600]{2,1,0:T(8,128)(2,1)S(1)}, u32[]{:S(2)}, u32[]{:S(2)}) collective-permute-start(bf16[1,200,1600]{2,1,0:T(8,128)(2,1)S(1)} %add_convert_fusion.4), channel_id=1, source_target_pairs={{0,8},{1,9},{2,6},{3,7},{4,12},{5,13},{6,2},{7,3},{8,0},{9,1},{10,... | collective-permute-start | bytes 1920008 | tf_op jit(solution)/shard_map/bgp/ppermute | solution.py:937
  837.0 28.9 %collective-permute-start.69 = (bf16[1,800,1600]{2,1,0:T(8,128)(2,1)}, bf16[1,800,1600]{2,1,0:T(8,128)(2,1)}, u32[]{:S(2)}, u32[]{:S(2)}) collective-permute-start(bf16[1,800,1600]{2,1,0:T(8,128)(2,1)} %bitcast.112.refs_2_), channel_id=1, source_target_pairs={{0,2},{1,3},{2,0},{3,1},{4,6},{5,7},{6,4},{7,5},{8,10},{9,11},{10,... | collective-permute-start | bytes 7680008 | tf_op jit(solution)/shard_map/bgc/ppermute | solution.py:937
  (90 other events, 1116.2 us)
